TPU v7x, 32 devices: a whole 2x2x4 slice. The times are simulated.
32 devices in a mesh: dp: 8 (over y, x, core), vocab: 4 (over z).
Axes of the slice: x: 2, y: 2, z: 4, core: 2. Of those that a mesh axis runs over, the one named last changes fastest.
Arguments:
- ids: int32 [8192], P(('dp', 'vocab')), may hold values from 0 to 50303
- targets: int32 [8192], P(('dp', 'vocab')), may hold values from 0 to 50303
- counted_mask: int32 [8192], P(('dp', 'vocab')), may hold values from 0 to 1
- lengths: int32 [32, 4], P(('dp', 'vocab')), may hold values from 1 to 192, 256 in all within a row
- table: bfloat16 [50304, 1024], P(('dp', 'vocab')), may hold values from -6 to 6
- position_table: bfloat16 [192, 1024], P(None, ('dp', 'vocab')), may hold values from -4 to 4
- layer_norm_gain: bfloat16 [3, 1024], P(None, ('dp', 'vocab')), may hold values from 0.5 to 1.5
- layer_norm_bias: bfloat16 [3, 1024], P(None, ('dp', 'vocab')), may hold values from -4 to 4
- query_key_value_weight: bfloat16 [1024, 3072], P(('dp', 'vocab')), may hold values from -0.1875 to 0.1875
- output_weight: bfloat16 [1024, 1024], P(('dp', 'vocab')), may hold values from -0.5 to 0.5
- up_weight: bfloat16 [1024, 4096], P(('dp', 'vocab')), may hold values from -0.1875 to 0.1875
- down_weight: bfloat16 [4096, 1024], P(('dp', 'vocab')), may hold values from -0.09375 to 0.09375
- biases: bfloat16 [9216], P(('dp', 'vocab')), may hold values from -4 to 4
- adapter_down: float32 [4, 1024, 4], replicated, may hold values from -0.1875 to 0.1875
- adapter_up: float32 [4, 4, 1024], replicated, may hold values from -0.1875 to 0.1875
- down_momentum: float32 [4, 1024, 4], replicated, may hold values from -0.078125 to 0.078125
- up_momentum: float32 [4, 4, 1024], replicated, may hold values from -0.078125 to 0.078125
Outputs:
- smoothed_loss_sum: float32 [], replicated
- loss_count: float32 [], replicated
- grad_norm: float32 [], replicated
- new_mom_down: float32 [4, 1024, 4], P(None, 'vocab')
- new_mom_up: float32 [4, 4, 1024], P(None, None, 'vocab')
- updated_down: float32 [4, 1024, 4], P(None, 'vocab')
- updated_up: float32 [4, 4, 1024], P(None, None, 'vocab')
- new_down_low: bfloat16 [4, 1024, 4], P(None, 'vocab')
- new_up_low: bfloat16 [4, 4, 1024], P(None, None, 'vocab')
Inputs may be any that keep to these rules, and one draw needn't show every extreme that they name: Token ids of the vocabulary. `targets`: target ids of the vocabulary. `lengths`: each row sums to 256; its longest length is exactly 192.
All inputs are finite; a program needn't handle non-finite values.
Results may differ from a plain program's by a relative error of at most 0.005.
Values may be sent and summed in bfloat16 or wider, within the bound.
A program may use at most 192 MiB of HBM per device.

v0:
```python
from functools import partial

import jax
import jax.numpy as jnp
from jax import lax
from jax.sharding import PartitionSpec as P

HEAD_DIM = 64
V = 50304


highest_precision = lax.Precision.HIGHEST
ln_eps = 1e-05
adapter_scale = 8.0
smooth = 0.1
clip_level = 1.0
momentum = 0.5
learning_rate = 0.5
coef_a = 3.4445
coef_b = -4.775
coef_c = 2.0315
score_scale = 0.125
masked_value = -1e30


def merged(x, axis, join):
    gathered = jax.tree.map(
        lambda a, kind: lax.all_gather(a.astype(kind), axis),
        x,
        jax.tree.map(lambda a: jnp.bfloat16 if a.dtype == jnp.float32 else a.dtype, x),
    )

    def take(source):
        return jax.tree.map(
            lambda a, own: lax.dynamic_index_in_dim(a, source, 0, False).astype(own.dtype),
            gathered,
            x,
        )

    return lax.fori_loop(
        1, lax.axis_size(axis), lambda source, state: join(state, take(source)), take(0)
    )


def dot_without_transpose(left_side, right_side, setting=None):
    return jnp.dot(left_side, right_side, precision=setting, preferred_element_type=jnp.float32)


def dot_last_axis(left_side, right_side, setting=None):
    return lax.dot_general(
        left_side,
        right_side,
        (((1,), (1,)), ((), ())),
        precision=setting,
        preferred_element_type=jnp.float32,
    )


def dot_first(left_side, right_side, setting=None):
    return lax.dot_general(
        left_side,
        right_side,
        (((0,), (0,)), ((), ())),
        precision=setting,
        preferred_element_type=jnp.float32,
    )


def rounded_values(values):
    return lax.optimization_barrier(values.astype(jnp.bfloat16)).astype(jnp.float32)


def layer_norm(values, gain, offset):
    center = values - jnp.mean(values, axis=-1, keepdims=True)
    spread = jnp.mean(center * center, axis=-1, keepdims=True)
    return center * lax.rsqrt(spread + ln_eps) * gain + offset


def layout(seq_lengths, row_count):
    seq_ends = jnp.cumsum(seq_lengths)
    seq_starts = seq_ends - seq_lengths
    places = jnp.arange(row_count, dtype=jnp.int32)
    segment = jnp.sum((places[:, None] >= seq_ends[None, :]).astype(jnp.int32), axis=1)
    member = segment[:, None] == jnp.arange(seq_lengths.shape[0], dtype=jnp.int32)[None, :]
    positions_in = places - jnp.sum(jnp.where(member, seq_starts[None, :], 0), axis=1)
    allowed_mask = (segment[:, None] == segment[None, :]) & (places[None, :] <= places[:, None])
    return (positions_in, allowed_mask)


def owner_rows(token_ids, piece_rows, group, vocab_pos):
    piece_index = token_ids // piece_rows
    owner = piece_index % group
    local = piece_index // group * piece_rows + token_ids % piece_rows
    return jnp.where(owner == vocab_pos, local, -1)


def attention_scores(query, key_rows, allowed_mask):
    scores = (
        jnp.einsum("shd,thd->hst", query, key_rows, preferred_element_type=jnp.float32)
        * score_scale
    )
    return jnp.where(allowed_mask[None], scores, masked_value)


def layer_forward(residual_initial, frozen_weights, adapter_down, adapter_up, allowed_mask):
    query_key_value_weight, output_weight, up_weight, down_weight, gains, shifts, bias_stack = (
        frozen_weights
    )
    gains = gains.astype(jnp.float32)
    shifts = shifts.astype(jnp.float32)
    bias_stack = bias_stack.astype(jnp.float32)
    width_size = output_weight.shape[0]
    hidden_units = up_weight.shape[1]
    row_count = residual_initial.shape[0]
    heads = width_size // HEAD_DIM
    first_normed = layer_norm(residual_initial, gains[0], shifts[0]).astype(jnp.bfloat16)
    first_plain = first_normed.astype(jnp.float32)
    joined_rows = (
        dot_without_transpose(first_normed, query_key_value_weight) + bias_stack[: 3 * width_size]
    )
    adapt_in = []
    projected = []
    for which_index in range(3):
        inner_product = dot_without_transpose(
            first_plain, adapter_down[which_index], highest_precision
        )
        adapt_in.append(inner_product)
        branch_output = joined_rows[
            :, which_index * width_size : (which_index + 1) * width_size
        ] + adapter_scale * dot_without_transpose(
            inner_product, adapter_up[which_index], highest_precision
        )
        projected.append(branch_output.astype(jnp.bfloat16).reshape(row_count, heads, HEAD_DIM))
    query, key_rows, value_rows = projected
    scores = attention_scores(query, key_rows, allowed_mask)
    top = jnp.max(scores, axis=-1, keepdims=True)
    expo = jnp.exp(scores - top)
    summed = jnp.sum(expo, axis=-1, keepdims=True)
    log_total = top + jnp.log(summed)
    probs = (expo / summed).astype(jnp.bfloat16)
    mixed_state = jnp.einsum("hst,thd->shd", probs, value_rows, preferred_element_type=jnp.float32)
    mixed_state = mixed_state.reshape(row_count, width_size).astype(jnp.bfloat16)
    mixed_plain = mixed_state.astype(jnp.float32)
    adapter_output = dot_without_transpose(mixed_plain, adapter_down[3], highest_precision)
    attended_rows = (
        dot_without_transpose(mixed_state, output_weight)
        + bias_stack[3 * width_size : 4 * width_size]
        + adapter_scale * dot_without_transpose(adapter_output, adapter_up[3], highest_precision)
    )
    stream_one = residual_initial + attended_rows
    normed_two = layer_norm(stream_one, gains[1], shifts[1]).astype(jnp.bfloat16)
    before_gelu = (
        dot_without_transpose(normed_two, up_weight)
        + bias_stack[4 * width_size : 4 * width_size + hidden_units]
    )
    activation = jax.nn.gelu(before_gelu, approximate=True).astype(jnp.bfloat16)
    stream_two = (
        stream_one
        + dot_without_transpose(activation, down_weight)
        + bias_stack[4 * width_size + hidden_units :]
    )
    final_state = layer_norm(stream_two, gains[2], shifts[2]).astype(jnp.bfloat16)
    kept_rows = (
        first_plain,
        adapt_in,
        query,
        key_rows,
        value_rows,
        log_total,
        mixed_plain,
        adapter_output,
        stream_one,
        before_gelu,
        stream_two,
    )
    return (final_state, kept_rows)


def layer_backward(
    final_gradient, kept_rows, backward_weights, adapter_down, adapter_up, allowed_mask
):
    output_weight, up_weight, down_weight, gains = backward_weights
    gains = gains.astype(jnp.float32)
    (
        first_plain,
        adapt_in,
        query,
        key_rows,
        value_rows,
        log_total,
        mixed_plain,
        adapter_output,
        stream_one,
        before_gelu,
        stream_two,
    ) = kept_rows
    row_count = query.shape[0]
    width_size = query.shape[1] * HEAD_DIM
    _, pull_three = jax.vjp(lambda values: layer_norm(values, gains[2], 0.0), stream_two)
    grad_two = pull_three(final_gradient)[0]
    grad_act = dot_last_axis(grad_two.astype(jnp.bfloat16), down_weight)
    _, pull_gelu = jax.vjp(partial(jax.nn.gelu, approximate=True), before_gelu)
    grad_pre = pull_gelu(grad_act)[0].astype(jnp.bfloat16)
    _, pull_two = jax.vjp(lambda values: layer_norm(values, gains[1], 0.0), stream_one)
    first_gradient = grad_two + pull_two(dot_last_axis(grad_pre, up_weight))[0]
    attention_gradient = first_gradient.astype(jnp.bfloat16)
    attention_scaled = adapter_scale * rounded_values(first_gradient)
    up_grads = [None, None, None, None]
    down_grads = [None, None, None, None]
    up_grads[3] = dot_first(adapter_output, attention_scaled, highest_precision)
    backward_output = dot_last_axis(attention_scaled, adapter_up[3], highest_precision)
    down_grads[3] = dot_first(mixed_plain, backward_output, highest_precision)
    mixed_gradient = dot_last_axis(attention_gradient, output_weight) + dot_last_axis(
        backward_output, adapter_down[3], highest_precision
    )
    grad_heads = mixed_gradient.astype(jnp.bfloat16).reshape(query.shape)
    probs = jnp.exp(attention_scores(query, key_rows, allowed_mask) - log_total)
    grad_value = jnp.einsum(
        "hst,shd->thd", probs.astype(jnp.bfloat16), grad_heads, preferred_element_type=jnp.float32
    )
    grad_probs = jnp.einsum(
        "shd,thd->hst", grad_heads, value_rows, preferred_element_type=jnp.float32
    )
    grad_scores = probs * (grad_probs - jnp.sum(probs * grad_probs, axis=-1, keepdims=True))
    grad_scores = grad_scores.astype(jnp.bfloat16)
    grad_query = (
        jnp.einsum("hst,thd->shd", grad_scores, key_rows, preferred_element_type=jnp.float32)
        * score_scale
    )
    grad_key = (
        jnp.einsum("hst,shd->thd", grad_scores, query, preferred_element_type=jnp.float32)
        * score_scale
    )
    for which_index, branch_gradient in enumerate((grad_query, grad_key, grad_value)):
        scaled_values = adapter_scale * rounded_values(
            branch_gradient.reshape(row_count, width_size)
        )
        up_grads[which_index] = dot_first(adapt_in[which_index], scaled_values, highest_precision)
        backward_input = dot_last_axis(scaled_values, adapter_up[which_index], highest_precision)
        down_grads[which_index] = dot_first(first_plain, backward_input, highest_precision)
    return (jnp.stack(down_grads), jnp.stack(up_grads))


def orthogonalize(matrices, sum_grams):
    grams = sum_grams(
        jnp.einsum(
            "mrd,msd->mrs",
            matrices,
            matrices,
            precision=highest_precision,
            preferred_element_type=jnp.float32,
        )
    )
    sizes = jnp.sqrt(jnp.trace(grams, axis1=1, axis2=2))[:, None, None] + 1e-07
    state = matrices / sizes
    grams = grams / (sizes * sizes)
    for turn_index in range(5):
        if turn_index:
            grams = sum_grams(
                jnp.einsum(
                    "mrd,msd->mrs",
                    state,
                    state,
                    precision=highest_precision,
                    preferred_element_type=jnp.float32,
                )
            )
        poly = coef_b * grams + coef_c * jnp.einsum(
            "mrs,mst->mrt",
            grams,
            grams,
            precision=highest_precision,
            preferred_element_type=jnp.float32,
        )
        state = coef_a * state + jnp.einsum(
            "mrs,msd->mrd",
            poly,
            state,
            precision=highest_precision,
            preferred_element_type=jnp.float32,
        )
    return state


def per_device(
    ids,
    targets,
    counted_mask,
    lengths,
    table,
    position_table,
    layer_norm_gain,
    layer_norm_bias,
    query_key_value_weight,
    output_weight,
    up_weight,
    down_weight,
    biases,
    adapter_down,
    adapter_up,
    down_momentum,
    up_momentum,
):
    gathered = (
        lax.all_gather(query_key_value_weight, ("dp", "vocab"), axis=0, tiled=True),
        lax.all_gather(output_weight, ("dp", "vocab"), axis=0, tiled=True),
        lax.all_gather(up_weight, ("dp", "vocab"), axis=0, tiled=True),
        lax.all_gather(down_weight, ("dp", "vocab"), axis=0, tiled=True),
        lax.all_gather(layer_norm_gain, ("dp", "vocab"), axis=1, tiled=True),
        lax.all_gather(layer_norm_bias, ("dp", "vocab"), axis=1, tiled=True),
        lax.all_gather(biases, ("dp", "vocab"), axis=0, tiled=True),
        lax.all_gather(position_table, ("dp", "vocab"), axis=1, tiled=True),
    )
    w_qkv_all, w_out_all, w_up_all, w_down_all, gains_all, shifts_all, bias_stack, positions_all = (
        gathered
    )
    row_count = ids.shape[0]
    width_size = w_out_all.shape[0]
    group = lax.axis_size("vocab")
    vocab_pos = lax.axis_index("vocab")
    piece_rows = table.shape[0]
    ids_all, target_all, mask_all = (
        lax.all_gather(ids, "vocab", axis=0, tiled=True),
        lax.all_gather(targets, "vocab", axis=0, tiled=True),
        lax.all_gather(counted_mask, "vocab", axis=0, tiled=True),
    )
    table_full = lax.all_gather(table, "dp", axis=0, tiled=True)
    vocab_rows = table_full.shape[0]
    local_ids = owner_rows(ids_all, piece_rows, group, vocab_pos)
    inside = local_ids >= 0
    picked_rows = table_full[jnp.clip(local_ids, 0, vocab_rows - 1)]
    picked_rows = jnp.where(inside[:, None], picked_rows, jnp.zeros_like(picked_rows))
    embedded = lax.psum_scatter(
        picked_rows.astype(jnp.float32).astype(jnp.bfloat16),
        "vocab",
        scatter_dimension=0,
        tiled=True,
    ).astype(jnp.float32)
    positions_in, allowed_mask = layout(lengths[0], row_count)
    residual_initial = embedded + positions_all[positions_in].astype(jnp.float32)
    frozen_weights = (w_qkv_all, w_out_all, w_up_all, w_down_all, gains_all, shifts_all, bias_stack)
    final_state, kept_rows = layer_forward(
        residual_initial, frozen_weights, adapter_down, adapter_up, allowed_mask
    )
    final_all = lax.all_gather(final_state, "vocab", axis=0, tiled=True)
    total_rows = final_all.shape[0]
    block = 512
    count_blocks = total_rows // block
    final_blocks = final_all.reshape(count_blocks, block, width_size)
    local_targets = owner_rows(target_all, piece_rows, group, vocab_pos).reshape(
        count_blocks, block
    )
    columns = jnp.arange(vocab_rows, dtype=jnp.int32)

    def head_stats(item):
        piece, local = item
        logits = dot_last_axis(piece, table_full)
        top = jnp.max(logits, axis=1)
        expsum = jnp.sum(jnp.exp(logits - top[:, None]), axis=1)
        target_logit = jnp.sum(jnp.where(columns[None, :] == local[:, None], logits, 0.0), axis=1)
        return (top, expsum, target_logit, jnp.sum(logits, axis=1))

    stats = lax.map(head_stats, (final_blocks, local_targets))
    stats = tuple((entry.reshape(total_rows) for entry in stats))

    def combine(first_part, second_part):
        larger = jnp.maximum(first_part[0], second_part[0])
        merged_sum = first_part[1] * jnp.exp(first_part[0] - larger) + second_part[1] * jnp.exp(
            second_part[0] - larger
        )
        return (larger, merged_sum, first_part[2] + second_part[2], first_part[3] + second_part[3])

    top, expsum, target_logit, logit_sum = merged(stats, "vocab", combine)
    log_total = top + jnp.log(expsum)
    row_loss = log_total - (1.0 - smooth) * target_logit - smooth * logit_sum / V
    mask_float = mask_all.astype(jnp.float32)
    own_start = vocab_pos * row_count
    loss_own = jnp.sum(lax.dynamic_slice_in_dim(mask_float * row_loss, own_start, row_count))
    count_own = jnp.sum(counted_mask.astype(jnp.float32))

    def head_grad(item):
        piece, local, lse_block, weight = item
        logits = dot_last_axis(piece, table_full)
        probs = jnp.exp(logits - lse_block[:, None])
        onehot = (columns[None, :] == local[:, None]).astype(jnp.float32)
        grad_logits = weight[:, None] * (probs - (1.0 - smooth) * onehot - smooth / V)
        return dot_without_transpose(grad_logits.astype(jnp.bfloat16), table_full)

    partial_rows = lax.map(
        head_grad,
        (
            final_blocks,
            local_targets,
            log_total.reshape(count_blocks, block),
            mask_float.reshape(count_blocks, block),
        ),
    )
    final_gradient = lax.psum_scatter(
        partial_rows.reshape(total_rows, width_size).astype(jnp.bfloat16),
        "vocab",
        scatter_dimension=0,
        tiled=True,
    ).astype(jnp.float32)
    backward_weights = (
        lax.all_gather(output_weight, ("dp", "vocab"), axis=0, tiled=True),
        lax.all_gather(up_weight, ("dp", "vocab"), axis=0, tiled=True),
        lax.all_gather(down_weight, ("dp", "vocab"), axis=0, tiled=True),
        lax.all_gather(layer_norm_gain, ("dp", "vocab"), axis=1, tiled=True),
    )
    down_gradient, up_gradient = layer_backward(
        final_gradient, kept_rows, backward_weights, adapter_down, adapter_up, allowed_mask
    )
    down_gradient, up_gradient, smoothed_loss_sum, loss_count = lax.psum(
        (down_gradient, up_gradient, loss_own, count_own), ("dp", "vocab")
    )
    grad_norm = jnp.sqrt(
        jnp.sum(down_gradient * down_gradient) + jnp.sum(up_gradient * up_gradient)
    )
    factor = jnp.minimum(1.0, clip_level / (grad_norm + 1e-06))
    new_mom_down = momentum * down_momentum + factor * down_gradient
    new_mom_up = momentum * up_momentum + factor * up_gradient
    stacked = jnp.concatenate([jnp.swapaxes(new_mom_down, 1, 2), new_mom_up], axis=0)
    share_fraction = stacked.shape[2] // group
    begin_index = vocab_pos * share_fraction
    orthogonal_update = orthogonalize(
        lax.dynamic_slice_in_dim(stacked, begin_index, share_fraction, 2),
        lambda grams: lax.psum(grams, "vocab"),
    )
    mom_down_part = lax.dynamic_slice_in_dim(new_mom_down, begin_index, share_fraction, 1)
    mom_up_part = lax.dynamic_slice_in_dim(new_mom_up, begin_index, share_fraction, 2)
    down_fresh = lax.dynamic_slice_in_dim(
        adapter_down, begin_index, share_fraction, 1
    ) - learning_rate * jnp.swapaxes(orthogonal_update[:4], 1, 2)
    up_fresh = (
        lax.dynamic_slice_in_dim(adapter_up, begin_index, share_fraction, 2)
        - learning_rate * orthogonal_update[4:]
    )
    return (
        smoothed_loss_sum,
        loss_count,
        grad_norm,
        mom_down_part,
        mom_up_part,
        down_fresh,
        up_fresh,
        down_fresh.astype(jnp.bfloat16),
        up_fresh.astype(jnp.bfloat16),
    )


def solution(mesh):
    placed = (
        P(("dp", "vocab")),
        P(("dp", "vocab")),
        P(("dp", "vocab")),
        P(("dp", "vocab"), None),
        P(("dp", "vocab"), None),
        P(None, ("dp", "vocab")),
        P(None, ("dp", "vocab")),
        P(None, ("dp", "vocab")),
        P(("dp", "vocab"), None),
        P(("dp", "vocab"), None),
        P(("dp", "vocab"), None),
        P(("dp", "vocab"), None),
        P(("dp", "vocab")),
        P(),
        P(),
        P(),
        P(),
    )
    return jax.shard_map(
        per_device,
        mesh=mesh,
        in_specs=placed,
        out_specs=(
            P(),
            P(),
            P(),
            P(None, "vocab", None),
            P(None, None, "vocab"),
            P(None, "vocab", None),
            P(None, None, "vocab"),
            P(None, "vocab", None),
            P(None, None, "vocab"),
        ),
        check_vma=False,
    )
```

profile of v0, /device:TPU:0, one launch (start us, length us, event | category | flops | bytes accessed | tf_op | source)
XLA Modules:
  0.0 1082.4 jit_solution(7209587581879092962)
XLA Ops:
  21.8 119.8 %all-gather.27.cloned.1.call-done = bf16[8,1572,1024]{2,1,0:T(8,128)(2,1)} async-done(((bf16[1,1572,1024]{2,1,0:T(8,128)(2,1)}), bf16[8,1572,1024]{2,1,0:T(8,128)(2,1)}) %all-gather.27.cloned.1.call-update) | async-done | bytes 25755664 | tf_op jit(solution)/shard_map/all_gather | solution.py:327
  141.6 27.2 %reshape.324 = bf16[12576,1024]{1,0:T(8,128)(2,1)} reshape(bf16[8,1572,1024]{2,1,0:T(8,128)(2,1)} %all-gather.27.cloned.1.call-done) | data formatting | bytes 51511296
  168.7 16.6 %gather_fusion = bf16[1024,1024]{1,0:T(8,128)(2,1)S(1)} fusion(bf16[12576,1024]{1,0:T(8,128)(2,1)} %reshape.324, s32[1024]{0:T(1024)S(1)} %fusion.136), kind=kCustom, calls=%fused_computation | custom fusion | bytes 4198400 | tf_op jit(solution)/shard_map/gather | solution.py:331
  189.8 42.2 %all-reduce = bf16[9216]{0:T(1024)(128)(2,1)S(1)} all-reduce(bf16[9216]{0:T(1024)(128)(2,1)S(1)} %dynamic-update-slice), channel_id=1, replica_groups=mesh['dp'=8,'vocab'=4] {'dp','vocab'}, use_global_device_ids=true, to_apply=%add | all-reduce | flops 9216 | bytes 36864
  232.1 73.1 %all_gather.62 = bf16[192,1024]{0,1:T(8,128)(2,1)S(1)} all-gather(bf16[192,32]{0,1:T(8,128)(2,1)S(1)} %copy-done.42), channel_id=1, replica_groups=mesh['dp'=8,'vocab'=4] {'dp','vocab'}, dimensions={1}, use_global_device_ids=true | all-gather | bytes 405504 | tf_op jit(solution)/shard_map/all_gather | solution.py:312
  305.4 64.3 %all-gather.3 = bf16[32,32,3]{1,2,0:T(4,128)(2,1)S(1)} all-gather(bf16[1,32,3]{1,2,0:T(4,128)(2,1)S(1)} %bitcast.325), channel_id=1, replica_groups=mesh['dp'=8,'vocab'=4] {'dp','vocab'}, dimensions={0}, use_global_device_ids=true | all-gather | bytes 6336 | tf_op jit(solution)/shard_map/all_gather | solution.py:309
  369.9 65.6 %all-gather.4 = bf16[32,32,3]{1,2,0:T(4,128)(2,1)S(1)} all-gather(bf16[1,32,3]{1,2,0:T(4,128)(2,1)S(1)} %bitcast.326), channel_id=1, replica_groups=mesh['dp'=8,'vocab'=4] {'dp','vocab'}, dimensions={0}, use_global_device_ids=true | all-gather | bytes 6336 | tf_op jit(solution)/shard_map/all_gather | solution.py:310
  472.7 31.2 %all-gather.23.cloned.1.call-done = bf16[4096,1024]{1,0:T(8,128)(2,1)} async-done(((bf16[128,1024]{1,0:T(8,128)(2,1)}), bf16[4096,1024]{1,0:T(8,128)(2,1)}) %all-gather.23.cloned.1.call-update) | async-done | bytes 8388624 | tf_op jit(solution)/shard_map/all_gather | solution.py:308
  532.2 26.1 %all-gather.25.cloned.1.call-done = bf16[1024,1024]{1,0:T(8,128)(2,1)} async-done(((bf16[256,1024]{1,0:T(8,128)(2,1)}), bf16[1024,1024]{1,0:T(8,128)(2,1)}) %all-gather.25.cloned.1.call-update) | async-done | bytes 2097168 | tf_op jit(solution)/shard_map/all_gather | solution.py:345
  558.3 71.4 %while.52 = (s32[]{:T(128)}, bf16[2,512]{1,0:T(2,128)(2,1)S(1)}, bf16[2,512]{1,0:T(2,128)(2,1)S(1)}, bf16[2,512]{1,0:T(2,128)(2,1)S(1)}, bf16[2,512]{1,0:T(2,128...) while((s32[]{:T(128)}, bf16[2,512]{1,0:T(2,128)(2,1)S(1)}, ...), condition=%wide.region_17.18_spmd.clone, body=%wide.region_12.17_spmd.clone.sunk | while | flops 13231962112 | bytes 78348904 | solution.py:363
  558.3 23.4 %fusion.271 = (f32[512]{0:T(512)S(1)}, f32[512,12576]{0,1:T(8,128)}) fusion(bf16[12576,1024]{1,0:T(8,128)(2,1)} %get-tuple-element.727, bf16[2,512,1024]{2,1,0:T(8,128)(2,1)} %get-tuple-element.726, s32[]{:T(128)} %get-tuple-element.711), kind=kOutput, calls=%fused_computation.302.clone.1 | convolution fusion | flops 13193330688 | bytes 52562432 | tf_op jit(solution)/shard_map/while/body/eval_jaxpr/dot_general | solution.py:50
  594.0 23.4 %fusion.271 = (f32[512]{0:T(512)S(1)}, f32[512,12576]{0,1:T(8,128)}) fusion(bf16[12576,1024]{1,0:T(8,128)(2,1)} %get-tuple-element.727, bf16[2,512,1024]{2,1,0:T(8,128)(2,1)} %get-tuple-element.726, s32[]{:T(128)} %get-tuple-element.711), kind=kOutput, calls=%fused_computation.302.clone.1 | convolution fusion | flops 13193330688 | bytes 52562432 | tf_op jit(solution)/shard_map/while/body/eval_jaxpr/dot_general | solution.py:50
  683.4 97.4 %while.53 = (s32[]{:T(128)}, bf16[2,512,1024]{2,1,0:T(8,128)(2,1)}, f32[2,512]{1,0:T(2,128)S(1)}, bf16[2,512,1024]{2,1,0:T(8,128)(2,1)}, bf16[12576,1024]{1,0:T(...) while((s32[]{:T(128)}, bf16[2,512,1024]{2,1,0:T(8,128)(2,1)}, ...), condition=%wide.region_25.26_spmd.clone, body=%wide.region_24.25_spmd.clone.sunk | while | flops 26418855936 | bytes 80432216 | solution.py:389
  683.6 26.8 %multiply_convert_fusion.clone.8 = bf16[512,12576]{0,1:T(8,128)(2,1)} fusion(bf16[12576,1024]{1,0:T(8,128)(2,1)} %get-tuple-element.787, s32[512]{0:T(512)S(1)} %bitcast.308, f32[512]{0:T(512)S(1)} %bitcast.306, f32[512]{0:T(512)S(1)} %bitcast.307, bf16[2,512,1024]{2,1,0:T(8,128)(2,1)} %get-tuple-element.786, ...), kind=kOutput, calls=%fused_computation.18.clone.clone.clone.clone.clone.1.clone.1 | convolution fusion | flops 13231964160 | bytes 39688704 | tf_op jit(solution)/shard_map/while/body/eval_jaxpr/dot_general | solution.py:50
  710.5 21.6 %bitcast_dynamic-update-slice_fusion.2 = bf16[2,512,1024]{2,1,0:T(8,128)(2,1)} fusion(bf16[2,512,1024]{2,1,0:T(8,128)(2,1)} %get-tuple-element.776, s32[]{:T(128)} %get-tuple-element.775, bf16[12576,1024]{1,0:T(8,128)(2,1)} %get-tuple-element.787, bf16[512,12576]{0,1:T(8,128)(2,1)} %multiply_convert_fusion.clone.8), kind=kOutput, calls=%fused_computation.26.clone.2 | convolution fusion | flops 13186891776 | bytes 40731136 | tf_op jit(solution)/shard_map/while/body/eval_jaxpr/dot_general | solution.py:46
  732.1 26.8 %multiply_convert_fusion.clone.8 = bf16[512,12576]{0,1:T(8,128)(2,1)} fusion(bf16[12576,1024]{1,0:T(8,128)(2,1)} %get-tuple-element.787, s32[512]{0:T(512)S(1)} %bitcast.308, f32[512]{0:T(512)S(1)} %bitcast.306, f32[512]{0:T(512)S(1)} %bitcast.307, bf16[2,512,1024]{2,1,0:T(8,128)(2,1)} %get-tuple-element.786, ...), kind=kOutput, calls=%fused_computation.18.clone.clone.clone.clone.clone.1.clone.1 | convolution fusion | flops 13231964160 | bytes 39688704 | tf_op jit(solution)/shard_map/while/body/eval_jaxpr/dot_general | solution.py:50
  758.9 21.6 %bitcast_dynamic-update-slice_fusion.2 = bf16[2,512,1024]{2,1,0:T(8,128)(2,1)} fusion(bf16[2,512,1024]{2,1,0:T(8,128)(2,1)} %get-tuple-element.776, s32[]{:T(128)} %get-tuple-element.775, bf16[12576,1024]{1,0:T(8,128)(2,1)} %get-tuple-element.787, bf16[512,12576]{0,1:T(8,128)(2,1)} %multiply_convert_fusion.clone.8), kind=kOutput, calls=%fused_computation.26.clone.2 | convolution fusion | flops 13186891776 | bytes 40731136 | tf_op jit(solution)/shard_map/while/body/eval_jaxpr/dot_general | solution.py:46
  783.0 40.7 %reduce-scatter.5.cloned.1.call-done = bf16[256,1024]{1,0:T(8,128)(2,1)} async-done(((bf16[1024,1024]{1,0:T(8,128)(2,1)}), bf16[256,1024]{1,0:T(8,128)(2,1)}) %reduce-scatter.5.cloned.1.call-update) | async-done | bytes 524304 | tf_op jit(solution)/shard_map/reduce_scatter | solution.py:398
  859.1 39.9 %all-reduce.1 = (f32[]{:T(128)}, f32[]{:T(128)}) all-reduce(f32[]{:T(128)} %dynamic-slice_reduce_fusion, f32[]{:T(128)} %convert_reduce_fusion.1), channel_id=1, replica_groups=mesh['dp'=8,'vocab'=4] {'dp','vocab'}, use_global_device_ids=true, to_apply=%region_21.22 | all-reduce | flops 2 | bytes 16 | tf_op jit(solution)/shard_map/psum | solution.py:413
  899.1 82.1 %all-reduce.5.cloned.1.call-done = (f32[4,1024,4]{1,2,0:T(4,128)}, f32[4,4,1024]{2,1,0:T(4,128)}) async-done(((f32[4,1024,4]{1,2,0:T(4,128)}, f32[4,4,1024]{2,1,0:T(4,128)}), (f32[4,1024,4]{1,2,0:T(4,128)}, f32[4,4,1024]{2,1,0:T(4,128)})) %all-reduce.5.cloned.1.call-update) | async-done | bytes 131088 | tf_op jit(solution)/shard_map/psum | solution.py:413
  987.5 17.7 %psum.67 = f32[8,4,4]{2,1,0:T(4,128)S(1)} all-reduce(f32[8,4,4]{2,1,0:T(4,128)S(1)} %fusion.179), channel_id=1, replica_groups=mesh['dp'=8,'vocab'=4] {'vocab'}, use_global_device_ids=true, to_apply=%region_36.37 | all-reduce | flops 128 | bytes 1024 | tf_op jit(solution)/shard_map/psum | solution.py:427
  1006.0 15.5 %psum.68 = f32[8,4,4]{2,1,0:T(4,128)S(1)} all-reduce(f32[8,4,4]{2,1,0:T(4,128)S(1)} %fusion.180), channel_id=1, replica_groups=mesh['dp'=8,'vocab'=4] {'vocab'}, use_global_device_ids=true, to_apply=%region_38.39 | all-reduce | flops 128 | bytes 1024 | tf_op jit(solution)/shard_map/psum | solution.py:427
  1022.1 16.3 %psum.69 = f32[8,4,4]{2,1,0:T(4,128)S(1)} all-reduce(f32[8,4,4]{2,1,0:T(4,128)S(1)} %fusion.181), channel_id=1, replica_groups=mesh['dp'=8,'vocab'=4] {'vocab'}, use_global_device_ids=true, to_apply=%region_39.40 | all-reduce | flops 128 | bytes 1024 | tf_op jit(solution)/shard_map/psum | solution.py:427
  1055.2 16.3 %psum.71 = f32[8,4,4]{2,1,0:T(4,128)S(1)} all-reduce(f32[8,4,4]{2,1,0:T(4,128)S(1)} %fusion.183), channel_id=1, replica_groups=mesh['dp'=8,'vocab'=4] {'vocab'}, use_global_device_ids=true, to_apply=%region_41.42 | all-reduce | flops 128 | bytes 1024 | tf_op jit(solution)/shard_map/psum | solution.py:427
  (334 shorter events, 224.2 us)
Async XLA Ops:
  8.0 133.6 %all-gather.27.cloned.1.call-start = ((), (), s32[]{:S(2)}) async-start(), calls=%async_computation.9 | async-start | bytes 29048832 | tf_op jit(solution)/shard_map/all_gather | solution.py:327
  8.7 428.6 %reduce-scatter.3.cloned.1.call-start = ((), (), s32[]{:S(2)}) async-start(), calls=%async_computation.2 | async-start | bytes 2621440 | tf_op jit(solution)/shard_map/reduce_scatter | solution.py:333
  185.4 120.0 %copy-start.56 = (bf16[3,32]{1,0:T(4,128)(2,1)S(1)}, bf16[3,32]{1,0:T(4,128)(2,1)}, u32[]{:S(2)}) copy-start(bf16[3,32]{1,0:T(4,128)(2,1)} %param.29) | copy-start | bytes 580
  185.4 184.5 %copy-start.57 = (bf16[3,32]{1,0:T(4,128)(2,1)S(1)}, bf16[3,32]{1,0:T(4,128)(2,1)}, u32[]{:S(2)}) copy-start(bf16[3,32]{1,0:T(4,128)(2,1)} %param.30) | copy-start | bytes 580
  185.4 250.2 %copy-start.62 = (s32[1,4]{1,0:T(1,128)S(1)}, s32[1,4]{1,0:T(1,128)}, u32[]{:S(2)}) copy-start(s32[1,4]{1,0:T(1,128)} %param.26) | copy-start | bytes 52
  187.0 254.9 %all-gather.17.cloned.1.call-start = ((), (), s32[]{:S(2)}) async-start(), calls=%async_computation.3 | async-start | bytes 6488064 | tf_op jit(solution)/shard_map/all_gather | solution.py:305
  187.6 272.4 %all-gather.19.cloned.1.call-start = ((), (), s32[]{:S(2)}) async-start(), calls=%async_computation.4 | async-start | bytes 2162688 | tf_op jit(solution)/shard_map/all_gather | solution.py:306
  188.2 276.2 %all-gather.21.cloned.1.call-start = ((), (), s32[]{:S(2)}) async-start(), calls=%async_computation.5 | async-start | bytes 8650752 | tf_op jit(solution)/shard_map/all_gather | solution.py:307
  188.8 315.2 %all-gather.23.cloned.1.call-start = ((), (), s32[]{:S(2)}) async-start(), calls=%async_computation.6 | async-start | bytes 8650752 | tf_op jit(solution)/shard_map/all_gather | solution.py:308
  189.5 368.8 %all-gather.25.cloned.1.call-start = ((), (), s32[]{:S(2)}) async-start(), calls=%async_computation.7 | async-start | bytes 2621440 | tf_op jit(solution)/shard_map/all_gather | solution.py:345
  513.5 310.1 %reduce-scatter.5.cloned.1.call-start = ((), (), s32[]{:S(2)}) async-start(), calls=%async_computation.8 | async-start | bytes 2621440 | tf_op jit(solution)/shard_map/reduce_scatter | solution.py:398
  558.3 124.4 %copy-start.43 = (f32[4,1,256]{2,1,0:T(1,128)S(1)}, f32[4,1,256]{2,1,0:T(1,128)}, u32[]{:S(2)}) copy-start(f32[4,1,256]{2,1,0:T(1,128)} %convert_element_type.339) | copy-start | bytes 12292
  558.3 125.0 %copy-start.31 = (f32[2,512]{1,0:T(2,128)S(1)}, f32[2,512]{1,0:T(2,128)}, u32[]{:S(2)}) copy-start(f32[2,512]{1,0:T(2,128)} %reshape.289) | copy-start | bytes 12292
  683.3 97.6 %copy-start.60 = (s32[256]{0:T(256)S(1)}, s32[256]{0:T(256)}, u32[]{:S(2)}) copy-start(s32[256]{0:T(256)} %param.25) | copy-start | bytes 3076
  683.3 98.2 %copy-start.22 = (f32[16,256]{1,0:T(8,128)S(1)}, f32[16,256]{1,0:T(8,128)}, u32[]{:S(2)}) copy-start(f32[16,256]{1,0:T(8,128)} %copy-done.21) | copy-start | bytes 49156
  683.4 98.2 %copy-start.28 = (f32[16,256]{1,0:T(8,128)S(1)}, f32[16,256]{1,0:T(8,128)}, u32[]{:S(2)}) copy-start(f32[16,256]{1,0:T(8,128)} %copy-done.27) | copy-start | bytes 49156
  683.4 140.3 %copy-start.5 = (f32[256,1024]{1,0:T(8,128)S(1)}, f32[256,1024]{1,0:T(8,128)}, u32[]{:S(2)}) copy-start(f32[256,1024]{1,0:T(8,128)} %copy-done.4) | copy-start | bytes 3145732
  683.4 140.2 %copy-start.26 = (f32[1,1024]{1,0:T(1,128)S(1)}, f32[1,1024]{1,0:T(1,128)}, u32[]{:S(2)}) copy-start(f32[1,1024]{1,0:T(1,128)} %copy-done.25) | copy-start | bytes 12292
  683.4 140.2 %copy-start.41 = (f32[256]{0:T(256)S(1)}, f32[256]{0:T(256)}, u32[]{:S(2)}) copy-start(f32[256]{0:T(256)} %copy-done.40) | copy-start | bytes 3076
  683.4 141.5 %copy-start.51 = (f32[256]{0:T(256)S(1)}, f32[256]{0:T(256)}, u32[]{:S(2)}) copy-start(f32[256]{0:T(256)} %copy-done.50) | copy-start | bytes 3076
  683.4 141.6 %copy-start.45 = (f32[256]{0:T(256)S(1)}, f32[256]{0:T(256)}, u32[]{:S(2)}) copy-start(f32[256]{0:T(256)} %copy-done.44) | copy-start | bytes 3076
  780.9 200.2 %all-reduce.5.cloned.1.call-start = ((), (), s32[]{:S(2)}) async-start(), calls=%async_computation.10 | async-start | bytes 262144 | tf_op jit(solution)/shard_map/psum | solution.py:413
  851.1 134.4 %copy-start.29 = (f32[4,4,1024]{2,1,0:T(4,128)S(1)}, f32[4,4,1024]{2,1,0:T(4,128)}, u32[]{:S(2)}) copy-start(f32[4,4,1024]{2,1,0:T(4,128)} %param.39) | copy-start | bytes 196612
  851.1 135.3 %copy-start.30 = (f32[4,1024,4]{1,2,0:T(4,128)S(1)}, f32[4,1024,4]{1,2,0:T(4,128)}, u32[]{:S(2)}) copy-start(f32[4,1024,4]{1,2,0:T(4,128)} %param.38) | copy-start | bytes 196612
  (48 other events, 565.0 us)
Sparse Core Ops, SparseCore 0:
  10.7 130.7 all-gather.26
  187.2 47.5 reduce-scatter.2
  513.6 44.6 all-gather.24
  781.0 42.5 reduce-scatter.4
Sparse Core Ops, SparseCore 1:
  190.8 94.0 all-gather.16
  288.1 56.3 all-gather.18
  347.6 76.3 all-gather.20
  427.3 76.6 all-gather.22
  859.2 121.9 all-reduce.4
where the time goes:
time: 1090 us; the launch traced here: 1080 us
  blocking collectives  449 us (41%)
  waiting for transfers between devices  303 us (28%)
  matrix products  208 us (19%)
  local copies, waits for them, and re-layouts  53.8 us (5%)
  other arithmetic  47.8 us (4%)
  between operations  19.4 us (2%)
    all_gather x1, waiting for transfers between devices, per_device(): table_full = lax.all_gather(table, 'dp', axis=0, tiled=True)  120 us
    dot_general x11, matrix products, dot_last_axis(): lax.dot_general(left_side, right_side, (((1,), (1,)), ((), ())), precisio...  119 us
    psum x1, waiting for transfers between devices, per_device(): lax.psum((down_gradient, up_gradient, loss_own, count_own), ('dp', 'vocab'))  82.1 us
    psum x5, blocking collectives, per_device(): lax.psum(grams, 'vocab')  81.4 us
    dot_general x14, matrix products, dot_without_transpose(): jnp.dot(left_side, right_side, precision=setting, preferred_element_type=...  74.6 us
    all_gather x1, blocking collectives, per_device(): lax.all_gather(position_table, ('dp', 'vocab'), axis=1, tiled=True)  73.1 us
    all_gather x1, blocking collectives, per_device(): lax.all_gather(layer_norm_bias, ('dp', 'vocab'), axis=1, tiled=True)  65.6 us
    all_gather x1, blocking collectives, per_device(): lax.all_gather(layer_norm_gain, ('dp', 'vocab'), axis=1, tiled=True)  64.3 us
  transfers between devices with their start and end apart: 9, of which 5 were waited for; matrix products, arithmetic and copies ran while one was open for 3% of the time, Pallas kernels for 0%

commit v1 on v0

--- a/solution.py
+++ b/solution.py
@@ -3,6 +3,8 @@
 import jax
 import jax.numpy as jnp
 from jax import lax
+from jax.experimental import pallas as pl
+from jax.experimental.pallas import tpu as pltpu
 from jax.sharding import PartitionSpec as P
 
 HEAD_DIM = 64
@@ -282,7 +284,7 @@
     return state
 
 
-def per_device(
+def per_device_general(
     ids,
     targets,
     counted_mask,
@@ -422,9 +424,8 @@
     stacked = jnp.concatenate([jnp.swapaxes(new_mom_down, 1, 2), new_mom_up], axis=0)
     share_fraction = stacked.shape[2] // group
     begin_index = vocab_pos * share_fraction
-    orthogonal_update = orthogonalize(
-        lax.dynamic_slice_in_dim(stacked, begin_index, share_fraction, 2),
-        lambda grams: lax.psum(grams, "vocab"),
+    orthogonal_update = lax.dynamic_slice_in_dim(
+        orthogonalize(stacked, lambda grams: grams), begin_index, share_fraction, 2
     )
     mom_down_part = lax.dynamic_slice_in_dim(new_mom_down, begin_index, share_fraction, 1)
     mom_up_part = lax.dynamic_slice_in_dim(new_mom_up, begin_index, share_fraction, 2)
@@ -448,7 +449,895 @@
     )
 
 
+MESH = pl.DeviceIdType.MESH
+CAP = 32
+
+
+def dot_nt(left_side, right_side, setting=None):
+    return dot_last_axis(left_side, right_side, setting)
+
+
+def position():
+    dp, z = lax.axis_index("dp"), lax.axis_index("vocab")
+    y, x, core = dp // 4, dp // 2 % 2, dp % 2
+
+    def place(y_at, x_at, core_at):
+        return y_at * 4 + x_at * 2 + core_at
+
+    along = (z, z // 2 * 2 + 1 - z % 2, (z + 2) % 4, (1 - z // 2) * 2 + 1 - z % 2)
+    return dp, z, y, x, core, place, along
+
+
+def meet_all(devices, group):
+    me = lax.axis_index("dp") * group + lax.axis_index("vocab")
+    barrier = pltpu.get_barrier_semaphore()
+
+    def signal(step, state):
+        other = lax.rem(me + step, devices)
+        pl.semaphore_signal(
+            barrier, inc=1, device_id=(other // group, other % group), device_id_type=MESH
+        )
+        return state
+
+    lax.fori_loop(1, devices, signal, 0)
+    pl.semaphore_wait(barrier, devices - 1)
+    return me
+
+
+def to_all(source_of, target, send_sems, recv_sems, devices, group, me):
+    def copy(step):
+        other = lax.rem(me + step, devices)
+        return pltpu.make_async_remote_copy(
+            source_of(other),
+            target.at[me],
+            send_sems.at[step],
+            recv_sems.at[step],
+            device_id=(other // group, other % group),
+            device_id_type=MESH,
+        )
+
+    def start():
+        def one(step, state):
+            copy(step).start()
+            return state
+
+        lax.fori_loop(1, devices, one, 0)
+
+    def arrive():
+        def one(step, state):
+            source = lax.rem(me + devices - step, devices)
+            pltpu.make_async_remote_copy(
+                target.at[source],
+                target.at[source],
+                send_sems.at[step],
+                recv_sems.at[step],
+                device_id=(source // group, source % group),
+                device_id_type=MESH,
+            ).wait_recv()
+            return state
+
+        lax.fori_loop(1, devices, one, 0)
+
+    def sent():
+        def one(step, state):
+            copy(step).wait_send()
+            return state
+
+        lax.fori_loop(1, devices, one, 0)
+
+    return start, arrive, sent
+
+
+def gather_kernel(row_counts, table_rows, devices, group, *refs):
+    count = len(row_counts)
+    token_row, token_col, table, table_turned = refs[:4]
+    ins = refs[4 : 4 + count]
+    refs = refs[4 + count :]
+    embedded, target_rows, table_sum, flags, table_other, turned_other = refs[:6]
+    outs = refs[6 : 6 + count]
+    (
+        send_sems,
+        recv_sems,
+        local_sems,
+        table_sems,
+        ask_sems,
+        row_sems,
+        sum_sems,
+        table_here,
+        selector,
+        rows_out,
+        rows_in,
+        ask_out,
+        ask_in,
+        sum_out,
+        sum_in,
+    ) = refs[6 + count :]
+    dp, z, y, x, core, place, along = position()
+    dp_x, dp_y = place(y, 1 - x, core), place(1 - y, x, core)
+    dp_core, dp_diagonal = place(y, x, 1 - core), place(1 - y, 1 - x, core)
+    peers = [(dp, along[k]) for k in (1, 2, 3)] + [(dp_x, z), (dp_y, z), (dp_core, z)]
+    load = pltpu.make_async_copy(table, table_here, table_sems.at[0])
+    load.start()
+    me = meet_all(devices, group)
+    mine = me
+    sent, kept, used = [], [], [0] * count
+
+    def piece(which, block):
+        rows = row_counts[which]
+        return outs[which].at[pl.ds(pl.multiple_of(block * rows, rows), rows)]
+
+    def send(which, block, peer, source=None):
+        copy = pltpu.make_async_remote_copy(
+            piece(which, block) if source is None else source,
+            piece(which, block),
+            send_sems.at[which, used[which]],
+            recv_sems.at[which, block],
+            device_id=peer,
+            device_id_type=MESH,
+        )
+        used[which] += 1
+        copy.start()
+        sent.append(copy)
+
+    def arrive(which, block):
+        pltpu.make_async_remote_copy(
+            ins[which],
+            piece(which, block),
+            send_sems.at[which, 0],
+            recv_sems.at[which, block],
+            device_id=peers[0],
+            device_id_type=MESH,
+        ).wait_recv()
+
+    def own(which):
+        for peer in peers:
+            send(which, mine, peer, ins[which])
+        copy = pltpu.make_async_copy(ins[which], piece(which, mine), local_sems.at[which])
+        copy.start()
+        kept.append(copy)
+
+    def line(which):
+        for k in (1, 2, 3):
+            block = dp * 4 + along[k]
+            arrive(which, block)
+            for peer in (dp_x, dp_y, dp_core):
+                send(which, block, (peer, z))
+
+    def side(which):
+        for k in range(4):
+            block_x, block_y = dp_x * 4 + along[k], dp_y * 4 + along[k]
+            arrive(which, block_y)
+            if k < 2:
+                send(which, block_y, (dp_x, z))
+            arrive(which, block_x)
+            if k >= 2:
+                send(which, block_x, (dp_y, z))
+            send(which, block_y, (dp_core, z))
+            send(which, block_x, (dp_core, z))
+
+    def diagonal(which):
+        for k in range(4):
+            block = dp_diagonal * 4 + along[k]
+            arrive(which, block)
+            send(which, block, (dp_core, z))
+
+    def other_core(which):
+        for y_at in range(2):
+            for x_at in range(2):
+                for z_at in range(4):
+                    arrive(which, place(y_at, x_at, 1 - core) * 4 + z_at)
+
+    own(0)
+    own(1)
+
+    tokens = token_row.shape[1]
+    wide = (tokens, tokens)
+    ids_row, ids_col = token_row[...], token_col[...]
+    across = lax.broadcasted_iota(jnp.int32, wide, 1).astype(jnp.float32)
+    down = lax.broadcasted_iota(jnp.int32, wide, 0).astype(jnp.float32)
+    owner_row, owner_col = jnp.zeros_like(ids_row), jnp.zeros_like(ids_col)
+    for device in range(1, devices):
+        owner_row += (ids_row >= float(device * table_rows)).astype(jnp.float32)
+        owner_col += (ids_col >= float(device * table_rows)).astype(jnp.float32)
+    equal = ids_col == ids_row
+    first_col = jnp.min(jnp.where(equal, across, float(tokens)), axis=1, keepdims=True)
+    first_row = jnp.min(jnp.where(equal, down, float(tokens)), axis=0, keepdims=True)
+    leads = jnp.where(first_row == across[:1], owner_row, -1.0)
+    slot_col = jnp.sum(
+        jnp.where((owner_col == leads) & (across < first_col), 1.0, 0.0), axis=1, keepdims=True
+    )
+    takes = lax.broadcasted_iota(jnp.int32, (devices, tokens), 0).astype(jnp.float32) == leads
+    local_row = jnp.where(takes, ids_row - owner_row * table_rows + 1.0, 0.0)
+    lanes = lax.broadcasted_iota(jnp.int32, (tokens, 128), 1).astype(jnp.float32)
+    asked = (
+        dot_without_transpose(
+            local_row, (slot_col == lanes).astype(jnp.float32), highest_precision
+        )
+        - 1.0
+    )
+    over = jnp.max(slot_col, axis=0, keepdims=True) >= float(CAP)
+    ask_lanes = lax.broadcasted_iota(jnp.int32, (devices, 128), 1)
+    asked = jnp.where(ask_lanes == 127, over.astype(jnp.float32), asked)
+    ask_out[...] = asked.reshape(devices, 1, 128)
+    ask_in[pl.ds(me, 1)] = ask_out[pl.ds(me, 1)]
+    start, ask_arrive, ask_sent = to_all(
+        lambda other: ask_out.at[other], ask_in, ask_sems.at[0], ask_sems.at[1], devices, group, me
+    )
+    start()
+    load.wait()
+
+    def add_up(step, total):
+        return total + jnp.sum(
+            table_here[pl.ds(pl.multiple_of(step * 128, 128), 128)].astype(jnp.float32),
+            axis=0,
+            keepdims=True,
+        )
+
+    own_sum = lax.fori_loop(
+        0, table_here.shape[0] // 128, add_up, jnp.zeros((1, table_here.shape[1]), jnp.float32)
+    )
+    sum_out[...] = own_sum
+    sum_in[pl.ds(me, 1)] = own_sum[None]
+    start, sum_arrive, sum_sent = to_all(
+        lambda other: sum_out, sum_in, sum_sems.at[0], sum_sems.at[1], devices, group, me
+    )
+    start()
+    ask_arrive()
+    asked_all = ask_in[...].reshape(devices, 128)
+    flags[...] = jnp.broadcast_to(
+        jnp.max(jnp.where(ask_lanes == 127, asked_all, 0.0), axis=0, keepdims=True).max(
+            axis=1, keepdims=True
+        ),
+        flags.shape,
+    )
+    square = (128, 128)
+    eye = (
+        lax.broadcasted_iota(jnp.int32, square, 0) == lax.broadcasted_iota(jnp.int32, square, 1)
+    ).astype(jnp.float32)
+    turned = dot_nt(eye, asked_all, highest_precision)
+    turned = jnp.round(turned)
+    row_lanes = lax.broadcasted_iota(jnp.int32, (CAP, table_here.shape[0]), 1).astype(jnp.float32)
+    for source in range(devices):
+        hot = turned[:CAP, source : source + 1] == row_lanes
+        selector[source * CAP : (source + 1) * CAP] = hot.astype(jnp.float32).astype(jnp.bfloat16)
+
+    def pick(step, state):
+        batch = 8 * CAP
+        picked = dot_without_transpose(
+            selector[pl.ds(pl.multiple_of(step * batch, batch), batch)], table_here[...]
+        )
+        rows_out[pl.ds(step * 8, 8)] = picked.astype(jnp.bfloat16).reshape(8, CAP, -1)
+        return state
+
+    lax.fori_loop(0, devices // 8, pick, 0)
+    rows_in[pl.ds(me, 1)] = rows_out[pl.ds(me, 1)]
+    start, rows_arrive, rows_sent = to_all(
+        lambda other: rows_out.at[other],
+        rows_in,
+        row_sems.at[0],
+        row_sems.at[1],
+        devices,
+        group,
+        me,
+    )
+    start()
+
+    line(0)
+    own(2)
+    line(1)
+    side(0)
+    own(3)
+    line(2)
+    side(1)
+    diagonal(0)
+    own(4)
+    line(3)
+    side(2)
+    diagonal(1)
+    swaps = []
+    for at, (here, there) in enumerate(((table, table_other), (table_turned, turned_other))):
+        copy = pltpu.make_async_remote_copy(
+            here,
+            there,
+            table_sems.at[1 + 2 * at],
+            table_sems.at[2 + 2 * at],
+            device_id=(dp_core, z),
+            device_id_type=MESH,
+        )
+        copy.start()
+        swaps.append(copy)
+
+    rows_arrive()
+    index_col = owner_col * CAP + slot_col
+    slots = lax.broadcasted_iota(jnp.int32, (tokens, devices * CAP), 1).astype(jnp.float32)
+    chosen = (index_col == slots).astype(jnp.float32).astype(jnp.bfloat16)
+    taken = dot_without_transpose(chosen, rows_in[...].reshape(devices * CAP, -1))
+    embedded[...] = taken[: tokens // 2]
+    target_rows[...] = taken[tokens // 2 :]
+    sum_arrive()
+    table_sum[...] = jnp.sum(sum_in[...], axis=0)
+
+    line(4)
+    side(3)
+    diagonal(2)
+    side(4)
+    diagonal(3)
+    diagonal(4)
+    for which in range(count):
+        other_core(which)
+    for copy in swaps:
+        copy.wait()
+    for copy in kept:
+        copy.wait()
+    for copy in sent:
+        copy.wait_send()
+    ask_sent()
+    sum_sent()
+    rows_sent()
+
+
+def gather_all(tokens, table, table_turned, table_rows, arrays):
+    count = len(arrays)
+    group = lax.axis_size("vocab")
+    devices = lax.axis_size("dp") * group
+    width = table.shape[1]
+    own_tokens = tokens.shape[0] // 2
+    anywhere, vmem = pl.BlockSpec(memory_space=pl.ANY), pl.BlockSpec(memory_space=pltpu.VMEM)
+    dma = pltpu.SemaphoreType.DMA
+    return pl.pallas_call(
+        partial(gather_kernel, [a.shape[0] for a in arrays], table_rows, devices, group),
+        out_shape=[
+            jax.ShapeDtypeStruct((own_tokens, width), jnp.float32),
+            jax.ShapeDtypeStruct((own_tokens, width), jnp.float32),
+            jax.ShapeDtypeStruct((1, width), jnp.float32),
+            jax.ShapeDtypeStruct((8, 128), jnp.float32),
+            jax.ShapeDtypeStruct(table.shape, table.dtype),
+            jax.ShapeDtypeStruct(table_turned.shape, table.dtype),
+        ]
+        + [jax.ShapeDtypeStruct((devices * a.shape[0],) + a.shape[1:], a.dtype) for a in arrays],
+        in_specs=[vmem, vmem] + [anywhere] * (2 + count),
+        out_specs=[vmem] * 4 + [anywhere] * (2 + count),
+        scratch_shapes=[
+            dma((count, devices)),
+            dma((count, devices)),
+            dma((count,)),
+            dma((5,)),
+            dma((2, devices)),
+            dma((2, devices)),
+            dma((2, devices)),
+            pltpu.VMEM(table.shape, table.dtype),
+            pltpu.VMEM((devices * CAP, table.shape[0]), jnp.bfloat16),
+            pltpu.VMEM((devices, CAP, width), jnp.bfloat16),
+            pltpu.VMEM((devices, CAP, width), jnp.bfloat16),
+            pltpu.VMEM((devices, 1, 128), jnp.float32),
+            pltpu.VMEM((devices, 1, 128), jnp.float32),
+            pltpu.VMEM((1, width), jnp.float32),
+            pltpu.VMEM((devices, 1, width), jnp.float32),
+        ],
+        name="gather_weights",
+        compiler_params=pltpu.CompilerParams(
+            collective_id=1, has_side_effects=True, vmem_limit_bytes=56 * 2**20
+        ),
+    )(
+        tokens.astype(jnp.float32)[None, :],
+        tokens.astype(jnp.float32)[:, None],
+        table,
+        table_turned,
+        *arrays,
+    )
+
+
+def pack_small(parts):
+    flat = jnp.concatenate([a.reshape(-1) for a in parts])
+    room = -(-flat.shape[0] // 8192) * 8192
+    return jnp.pad(flat, (0, room - flat.shape[0])).reshape(16, -1)
+
+
+def unpack_small(packed, shapes):
+    flat = packed.reshape(-1, 16 * packed.shape[1])
+    out, at = [], 0
+    for shape in shapes:
+        size = 1
+        for n in shape:
+            size *= n
+        piece = flat[:, at : at + size].reshape((-1,) + shape)
+        at += size
+        out.append(jnp.moveaxis(piece, 0, -2).reshape(shape[:-1] + (-1,)))
+    return out
+
+
+def head_kernel(table_rows, chunks, own, tab_a, turn_a, tab_b, turn_b, mean_out, lse_out, *refs):
+    (
+        tab,
+        turn,
+        score_a,
+        score_b,
+        total,
+        hidden,
+        part,
+        part_lse,
+        got,
+        got_lse,
+        load_sems,
+        send_sems,
+        recv_sems,
+        back_send,
+        back_recv,
+    ) = refs
+    dp, z, y, x, core, place, along = position()
+    pad_rows = tab_a.shape[0]
+    width, tile = own.shape[1], own.shape[0]
+    dev_x, dev_y = (place(y, 1 - x, core), z), (place(1 - y, x, core), z)
+    dev_z = [None] + [(dp, along[k]) for k in (1, 2, 3)]
+    peers = [dev_x, dev_y] + dev_z[1:]
+    loads = []
+    for at, (source, target) in enumerate(
+        (
+            (own, hidden.at[0]),
+            (tab_a, tab.at[pl.ds(0, pad_rows)]),
+            (tab_b, tab.at[pl.ds(pad_rows, pad_rows)]),
+            (turn_a, turn.at[:, pl.ds(0, pad_rows)]),
+            (turn_b, turn.at[:, pl.ds(pad_rows, pad_rows)]),
+        )
+    ):
+        copy = pltpu.make_async_copy(source, target, load_sems.at[at])
+        copy.start()
+        loads.append(copy)
+    barrier = pltpu.get_barrier_semaphore()
+    for peer in peers:
+        pl.semaphore_signal(barrier, inc=1, device_id=peer, device_id_type=MESH)
+    pl.semaphore_wait(barrier, len(peers))
+    loads[0].wait()
+
+    def give(source, target, peer):
+        return pltpu.make_async_remote_copy(
+            hidden.at[source],
+            hidden.at[target],
+            send_sems.at[target],
+            recv_sems.at[target],
+            device_id=peer,
+            device_id_type=MESH,
+        )
+
+    gives = [give(0, 4 * k, dev_z[k]) for k in (1, 2, 3)]
+    forwards = {}
+    for k in range(4):
+        forwards[4 * k] = [give(4 * k, 4 * k + 1, dev_x), give(4 * k, 4 * k + 2, dev_y)]
+        if k < 2:
+            forwards[4 * k + 2] = [give(4 * k + 2, 4 * k + 3, dev_x)]
+        else:
+            forwards[4 * k + 1] = [give(4 * k + 1, 4 * k + 3, dev_y)]
+    for copy in forwards[0] + gives:
+        copy.start()
+
+    def tile_comes(t, parity):
+        for at in range(1, 16):
+            if at % 2 != parity:
+                continue
+
+            @pl.when(t == at)
+            def _(at=at):
+                give(0, at, dev_x).wait_recv()
+                for copy in forwards.get(at, []):
+                    copy.start()
+
+    def back(t, slot, peer):
+        return [
+            pltpu.make_async_remote_copy(
+                source.at[t],
+                target.at[slot],
+                back_send.at[kind, slot],
+                back_recv.at[kind, slot],
+                device_id=peer,
+                device_id_type=MESH,
+            )
+            for kind, (source, target) in enumerate(((part, got), (part_lse, got_lse)))
+        ]
+
+    backs = {}
+    for k in range(4):
+        backs[4 * k + 3] = back(4 * k + 3, 8 + k, dev_x if k < 2 else dev_y)
+        backs[4 * k + 1] = back(4 * k + 1, k, dev_x)
+        backs[4 * k + 2] = back(4 * k + 2, 4 + k, dev_y)
+        if k:
+            backs[4 * k] = back(4 * k, 11 + k, dev_z[k])
+
+    def back_start(t):
+        for copy in backs[t]:
+            copy.start()
+
+    def back_wait(slot):
+        for copy in back(0, slot, dev_x):
+            copy.wait_recv()
+
+    def merge(t, slots):
+        for slot in slots:
+            back_wait(slot)
+        levels = [part_lse[t]] + [got_lse[slot] for slot in slots]
+        top = levels[0]
+        for level in levels[1:]:
+            top = jnp.maximum(top, level)
+        shares = [jnp.exp(level - top) for level in levels]
+        whole = sum(shares[1:], shares[0])
+        shares = [share / whole for share in shares]
+        part_lse[t] = top + jnp.log(whole)
+
+        def rows(step, state):
+            at = pl.ds(pl.multiple_of(step * 128, 128), 128)
+            mixed = part[t, at].astype(jnp.float32) * shares[0]
+            for slot, share in zip(slots, shares[1:], strict=True):
+                mixed += got[slot, at].astype(jnp.float32) * share
+            part[t, at] = mixed.astype(jnp.bfloat16)
+            return state
+
+        lax.fori_loop(0, width // 128, rows, 0)
+
+    def merge_middle(k):
+        t = 4 * k + 2 if k < 2 else 4 * k + 1
+        merge(t, [8 + k])
+        back_start(t)
+
+    def merge_column(k):
+        merge(4 * k, [k, 4 + k])
+        if k:
+            back_start(4 * k)
+
+    after = {}
+    for k in range(4):
+        after.setdefault(4 * k + 1 if k < 2 else 4 * k + 2, []).append(
+            partial(back_start, 4 * k + 1 if k < 2 else 4 * k + 2)
+        )
+        after.setdefault(4 * k + 3, []).append(partial(back_start, 4 * k + 3))
+    late = []
+    for k in range(4):
+        for delay, event in ((3, merge_middle), (7, merge_column)):
+            at = 4 * k + 3 + delay
+            if at < 16:
+                after.setdefault(at, []).append(partial(event, k))
+            else:
+                late.append((at, partial(event, k)))
+    late = [event for _, event in sorted(late, key=lambda entry: entry[0])]
+
+    def tile_done(t, parity):
+        for at in sorted(after):
+            if at % 2 != parity:
+                continue
+
+            @pl.when(t == at)
+            def _(at=at):
+                for event in after[at]:
+                    event()
+
+    for copy in loads[1:]:
+        copy.wait()
+    starts = [sum(chunks[:at]) for at in range(len(chunks))]
+    low = jnp.full((8, tile), -jnp.inf, jnp.float32)
+
+    def scores_of(rows, at, score, top):
+        begin, size = starts[at], chunks[at]
+        values = dot_nt(tab[begin : begin + size], rows)
+        score[begin : begin + size] = values
+        cuts = [(begin, begin + size, False)]
+        for half in range(2):
+            edge = half * pad_rows + table_rows // 8 * 8
+            stop = (half + 1) * pad_rows
+            if begin <= edge < begin + size:
+                cuts = [(begin, edge, False), (edge, min(stop, begin + size), True)]
+                if stop < begin + size:
+                    cuts.append((stop, begin + size, False))
+        for first, last, masked in cuts:
+            if first == last:
+                continue
+            cut = values[first - begin : last - begin]
+            if masked:
+                row = lax.broadcasted_iota(jnp.int32, cut.shape, 0)
+                cut = jnp.where(row < table_rows % 8, cut, masked_value)
+                score[first:last] = cut
+            top = jnp.maximum(top, jnp.max(cut.reshape(-1, 8, tile), axis=0))
+        return top
+
+    def half_step(t, parity, score, score_next, top):
+        after_t = jnp.minimum(t + 1, 15)
+        tile_comes(t + 1, 1 - parity)
+        rows = hidden[after_t]
+        peak = jnp.max(top, axis=0, keepdims=True)
+        summed = jnp.zeros((8, tile), jnp.float32)
+        top_next = low
+        for at in range(len(chunks)):
+            begin, size = starts[at], chunks[at]
+            expo = jnp.exp(score[begin : begin + size] - peak)
+            summed += jnp.sum(expo.reshape(-1, 8, tile), axis=0)
+            top_next = scores_of(rows, at, score_next, top_next)
+            product = dot_without_transpose(
+                turn[:, begin : begin + size], expo.astype(jnp.bfloat16)
+            )
+            if at == 0:
+                total[...] = product
+            else:
+                total[...] += product
+        denominator = jnp.sum(summed, axis=0, keepdims=True)
+        part[t] = (total[...] * (1.0 / denominator)).astype(jnp.bfloat16)
+        part_lse[t] = peak + jnp.log(denominator)
+        tile_done(t, parity)
+        return top_next
+
+    top = low
+    for at in range(len(chunks)):
+        top = scores_of(hidden[0], at, score_a, top)
+
+    def two_steps(step, top):
+        top = half_step(2 * step, 0, score_a, score_b, top)
+        return half_step(2 * step + 1, 1, score_b, score_a, top)
+
+    lax.fori_loop(0, 8, two_steps, top)
+    for event in late:
+        event()
+    merge(0, [12, 13, 14])
+    mean_out[...] = part[0]
+    lse_out[...] = part_lse[0]
+    for copies in [gives] + list(forwards.values()) + list(backs.values()):
+        for copy in copies:
+            copy.wait_send()
+
+
+def head(final_state, table_rows, tables):
+    tile, width = final_state.shape
+    pad_rows = tables[0].shape[0]
+    both = 2 * pad_rows
+    chunks = [both // 256 // 4 * 256] * 4
+    chunks[0] += both - sum(chunks)
+    anywhere, vmem = pl.BlockSpec(memory_space=pl.ANY), pl.BlockSpec(memory_space=pltpu.VMEM)
+    dma = pltpu.SemaphoreType.DMA
+    return pl.pallas_call(
+        partial(head_kernel, table_rows, chunks),
+        out_shape=[
+            jax.ShapeDtypeStruct((width, tile), jnp.bfloat16),
+            jax.ShapeDtypeStruct((1, tile), jnp.float32),
+        ],
+        in_specs=[anywhere] * 5,
+        out_specs=[vmem] * 2,
+        scratch_shapes=[
+            pltpu.VMEM((both, width), jnp.bfloat16),
+            pltpu.VMEM((width, both), jnp.bfloat16),
+            pltpu.VMEM((both, tile), jnp.float32),
+            pltpu.VMEM((both, tile), jnp.float32),
+            pltpu.VMEM((width, tile), jnp.float32),
+            pltpu.VMEM((16, tile, width), jnp.bfloat16),
+            pltpu.VMEM((16, width, tile), jnp.bfloat16),
+            pltpu.VMEM((16, 1, tile), jnp.float32),
+            pltpu.VMEM((15, width, tile), jnp.bfloat16),
+            pltpu.VMEM((15, 1, tile), jnp.float32),
+            dma((5,)),
+            dma((16,)),
+            dma((16,)),
+            dma((2, 15)),
+            dma((2, 15)),
+        ],
+        name="head",
+        compiler_params=pltpu.CompilerParams(
+            collective_id=2, has_side_effects=True, vmem_limit_bytes=62 * 2**20
+        ),
+    )(final_state, *tables)
+
+
+def update_kernel(devices, group, grads, momenta, weights, new_momenta, new_weights, numbers, *refs):
+    parts, whole, piece, sems, back_sems = refs
+    me = meet_all(devices, group)
+    z = lax.axis_index("vocab")
+    parts[pl.ds(me, 1)] = grads[pl.ds(me, 1)]
+    start, arrive, sent = to_all(
+        lambda other: grads.at[other], parts, sems.at[0], sems.at[1], devices, group, me
+    )
+    start()
+    arrive()
+    summed = parts[0]
+    for source in range(1, devices):
+        summed += parts[source]
+    width = momenta.shape[1]
+    piece[...] = summed[:, :width]
+    whole[pl.ds(me, 1)] = summed[None, :, :width]
+    start, back_arrive, back_sent = to_all(
+        lambda other: piece, whole, back_sems.at[0], back_sems.at[1], devices, group, me
+    )
+    start()
+    back_arrive()
+    gradient = whole[...].reshape(devices, width)
+    squares = jnp.sum(jnp.sum(gradient * gradient, axis=0, keepdims=True), axis=1, keepdims=True)
+    norm = jnp.sqrt(squares)
+    factor = jnp.minimum(1.0, clip_level / (norm + 1e-06))
+    state = momentum * momenta[...] + factor * gradient
+    share = new_momenta.shape[1]
+    columns = pl.ds(pl.multiple_of(z * share, share), share)
+    whole[...] = state.reshape(devices, 1, width)
+    new_momenta[...] = whole[:, 0, columns]
+    square = (devices, devices)
+    row = lax.broadcasted_iota(jnp.int32, square, 0)
+    column = lax.broadcasted_iota(jnp.int32, square, 1)
+    rank = 4
+    blocks = row // rank == column // rank
+
+    def gram_of(matrix):
+        return jnp.where(blocks, dot_nt(matrix, matrix, highest_precision), 0.0)
+
+    grams = gram_of(state)
+    diagonal = jnp.sum(jnp.where(row == column, grams, 0.0), axis=0, keepdims=True)
+    traces = jnp.sum(jnp.where(blocks, diagonal, 0.0), axis=1, keepdims=True)
+    sizes = jnp.sqrt(traces) + 1e-07
+    state = state / sizes
+    grams = grams / (sizes * sizes)
+    for turn_index in range(5):
+        if turn_index:
+            grams = gram_of(state)
+        poly = coef_b * grams + coef_c * dot_without_transpose(grams, grams, highest_precision)
+        state = coef_a * state + dot_without_transpose(poly, state, highest_precision)
+    whole[...] = (weights[...] - learning_rate * state).reshape(devices, 1, width)
+    new_weights[...] = whole[:, 0, columns]
+    lanes = lax.broadcasted_iota(jnp.int32, (1, 128), 1)
+    numbers[...] = jnp.where(lanes == 2, norm, summed[:, width:])
+    sent()
+    back_sent()
+
+
+def update(grads, momenta, weights):
+    group = lax.axis_size("vocab")
+    devices = lax.axis_size("dp") * group
+    width = momenta.shape[1]
+    vmem = pl.BlockSpec(memory_space=pltpu.VMEM)
+    dma = pltpu.SemaphoreType.DMA
+    small = jax.ShapeDtypeStruct((devices, width // group), jnp.float32)
+    return pl.pallas_call(
+        partial(update_kernel, devices, group),
+        out_shape=[small, small, jax.ShapeDtypeStruct((1, 128), jnp.float32)],
+        in_specs=[vmem] * 3,
+        out_specs=[vmem] * 3,
+        scratch_shapes=[
+            pltpu.VMEM(grads.shape, jnp.float32),
+            pltpu.VMEM((devices, 1, width), jnp.float32),
+            pltpu.VMEM((1, width), jnp.float32),
+            dma((2, devices)),
+            dma((2, devices)),
+        ],
+        name="update",
+        compiler_params=pltpu.CompilerParams(collective_id=3, has_side_effects=True),
+    )(grads, momenta, weights)
+
+
+def stack_adapters(down, up):
+    return jnp.concatenate([jnp.swapaxes(down, 1, 2), up], axis=0).reshape(-1, up.shape[2])
+
+
+def per_device(
+    ids,
+    targets,
+    counted_mask,
+    lengths,
+    table,
+    position_table,
+    layer_norm_gain,
+    layer_norm_bias,
+    query_key_value_weight,
+    output_weight,
+    up_weight,
+    down_weight,
+    biases,
+    adapter_down,
+    adapter_up,
+    down_momentum,
+    up_momentum,
+):
+    every = (
+        ids,
+        targets,
+        counted_mask,
+        lengths,
+        table,
+        position_table,
+        layer_norm_gain,
+        layer_norm_bias,
+        query_key_value_weight,
+        output_weight,
+        up_weight,
+        down_weight,
+        biases,
+        adapter_down,
+        adapter_up,
+        down_momentum,
+        up_momentum,
+    )
+    table_rows = table.shape[0]
+    row_count = ids.shape[0]
+    table = jnp.pad(table, ((0, -table_rows % 128), (0, 0)))
+    table_turned = table.T
+    tokens = jnp.concatenate([ids, jnp.where(counted_mask > 0, targets, ids)])
+    small = (position_table, layer_norm_gain, layer_norm_bias, biases)
+    (
+        embedded,
+        target_rows,
+        table_sum,
+        flags,
+        table_other,
+        turned_other,
+        packed,
+        w_qkv_all,
+        w_out_all,
+        w_up_all,
+        w_down_all,
+    ) = gather_all(
+        tokens,
+        table,
+        table_turned,
+        table_rows,
+        (pack_small(small), query_key_value_weight, output_weight, up_weight, down_weight),
+    )
+
+    def go_on():
+        positions_all, gains_all, shifts_all, bias_stack = unpack_small(
+            packed, [a.shape for a in small]
+        )
+        positions_in, allowed_mask = layout(lengths[0], row_count)
+        residual_initial = embedded + positions_all[positions_in].astype(jnp.float32)
+        frozen_weights = (
+            w_qkv_all,
+            w_out_all,
+            w_up_all,
+            w_down_all,
+            gains_all,
+            shifts_all,
+            bias_stack,
+        )
+        final_state, kept_rows = layer_forward(
+            residual_initial, frozen_weights, adapter_down, adapter_up, allowed_mask
+        )
+        mean_rows, log_total = head(
+            final_state, table_rows, (table, table_turned, table_other, turned_other)
+        )
+        mean_rows = mean_rows.T.astype(jnp.float32)
+        log_total = log_total[0]
+        state_float = final_state.astype(jnp.float32)
+        uniform = (smooth / V) * table_sum
+        pulled = (1.0 - smooth) * target_rows + uniform
+        row_loss = log_total - jnp.sum(state_float * pulled, axis=1)
+        mask_float = counted_mask.astype(jnp.float32)
+        loss_own = jnp.sum(mask_float * row_loss)
+        count_own = jnp.sum(mask_float)
+        final_gradient = mask_float[:, None] * (mean_rows - pulled)
+        backward_weights = (w_out_all, w_up_all, w_down_all, gains_all)
+        down_gradient, up_gradient = layer_backward(
+            final_gradient, kept_rows, backward_weights, adapter_down, adapter_up, allowed_mask
+        )
+        grads = stack_adapters(down_gradient, up_gradient)
+        extra = jnp.zeros((grads.shape[0], 128), jnp.float32)
+        extra = extra.at[:, 0].set(loss_own).at[:, 1].set(count_own)
+        grads = jnp.concatenate([grads, extra], axis=1)[:, None, :]
+        new_momenta, new_weights, numbers = update(
+            grads,
+            stack_adapters(down_momentum, up_momentum),
+            stack_adapters(adapter_down, adapter_up),
+        )
+
+        def split(stacked):
+            stacked = stacked.reshape(2, -1, adapter_up.shape[1], stacked.shape[1])
+            return jnp.swapaxes(stacked[0], 1, 2), stacked[1]
+
+        mom_down, mom_up = split(new_momenta)
+        down_fresh, up_fresh = split(new_weights)
+        return (
+            numbers[0, 0],
+            numbers[0, 1],
+            numbers[0, 2],
+            mom_down,
+            mom_up,
+            down_fresh,
+            up_fresh,
+            down_fresh.astype(jnp.bfloat16),
+            up_fresh.astype(jnp.bfloat16),
+        )
+
+    return lax.cond(flags[0, 0] > 0.0, lambda: per_device_general(*every), go_on)
+
+
 def solution(mesh):
+    fast = dict(mesh.shape) == {"dp": 8, "vocab": 4}
     placed = (
         P(("dp", "vocab")),
         P(("dp", "vocab")),
@@ -469,7 +1358,7 @@
         P(),
     )
     return jax.shard_map(
-        per_device,
+        per_device if fast else per_device_general,
         mesh=mesh,
         in_specs=placed,
         out_specs=(

time: 1090 us -> 653 us (0.60)
  blocking collectives: 449 us -> 0 us
  Pallas kernels: 0 us -> 446 us
  waiting for transfers between devices: 303 us -> 0 us
  matrix products: 208 us -> 83.3 us
  other arithmetic: 47.8 us -> 21.5 us
  local copies, waits for them, and re-layouts: 53.8 us -> 71.1 us
  loops' own time: 0.78 us -> 13.1 us
    pallas_call x0 -> x3, Pallas kernels: none -> 446 us  [the longest x1 231 us: head(): pl.pallas_call(partial(head_kernel, table_rows, chunks), out_shape=[jax.S...]
    all_gather x10 -> x0, blocking collectives: 286 us -> none  [the longest x1 73.1 us: per_device(): lax.all_gather(position_table, ('dp', 'vocab'), axis=1, tiled=True)]
    all_gather x6 -> x0, waiting for transfers between devices: 177 us -> none  [the longest x1 120 us: per_device(): table_full = lax.all_gather(table, 'dp', axis=0, tiled=True)]
    psum x6 -> x0, blocking collectives: 121 us -> none  [the longest x5 81.4 us: per_device(): lax.psum(grams, 'vocab')]
    dot_general x11 -> x7, matrix products: 119 us -> 18.2 us  [dot_last_axis(): lax.dot_general(left_side, right_side, (((1,), (1,)), ((), ())), precisio...]
    psum x1 -> x0, waiting for transfers between devices: 82.1 us -> none  [per_device(): lax.psum((down_gradient, up_gradient, loss_own, count_own), ('dp', 'vocab'))]
    unnamed x1 -> x0, blocking collectives: 42.2 us -> none
    reduce_scatter x2 -> x0, waiting for transfers between devices: 40.7 us -> none  [the longest x1 40.7 us: per_device(): lax.psum_scatter(partial_rows.reshape(total_rows, width_size).astype(jnp....]
  transfers between devices with their start and end apart: 9 -> 0, of which waited for: 5 -> 0; matrix products, arithmetic and copies ran while one was open for 3% -> 0% of each run, Pallas kernels for 0% -> 0%
where the time goes in v1:
time: 653 us; the launch traced here: 650 us
  Pallas kernels  446 us (68%)
  matrix products  83.3 us (13%)
  local copies, waits for them, and re-layouts  71.1 us (11%)
  other arithmetic  21.5 us (3%)
  between operations  15 us (2%)
  loops' own time  13.1 us (2%)
    pallas_call x1, Pallas kernels, head(): pl.pallas_call(partial(head_kernel, table_rows, chunks), out_shape=[jax.S...  231 us
    pallas_call x1, Pallas kernels, gather_all(): pl.pallas_call(partial(gather_kernel, [a.shape[0] for a in arrays], table...  185 us
    dot_general x12, matrix products, dot_without_transpose(): jnp.dot(left_side, right_side, precision=setting, preferred_element_type=...  41.8 us
    pallas_call x1, Pallas kernels, update(): pl.pallas_call(partial(update_kernel, devices, group), out_shape=[small,...  29.2 us
    dot_general x7, matrix products, dot_last_axis(): lax.dot_general(left_side, right_side, (((1,), (1,)), ((), ())), precisio...  18.2 us
    unnamed x124, local copies, waits for them, and re-layouts  13.6 us
    unnamed x1, loops' own time  13.1 us

profile of v1, /device:TPU:0, one launch (start us, length us, event | category | flops | bytes accessed | tf_op | source)
XLA Modules:
  0.0 649.8 jit_solution(16261300255880904067)
XLA Ops:
  7.2 5.4 copy.248
  12.5 4.1 pad_bitcast_fusion
  16.7 5.7 copy.251.refs_2_
  31.1 3.4 concatenate.55
  37.2 185.1 %gather_weights.1 = (f32[256,1024]{1,0:T(8,128)}, f32[256,1024]{1,0:T(8,128)}, f32[1,1024]{1,0:T(1,128)}, f32[8,128]{1,0:T(8,128)}, bf16[1664,1024]{1,0:T(8,128)...) custom-call(f32[1,512]{1,0:T(1,128)} %add_convert_fusion.22.refs_0_,, ...), custom_call_target="tpu_custom_call" | custom-call | tf_op jit(solution)/shard_map/gather_weights/pallas_call | solution.py:787
  224.2 417.2 %conditional.4 = (f32[]{:T(128)}, f32[]{:T(128)}, f32[]{:T(128)}, f32[4,256,4]{1,2,0:T(4,128)S(1)}, f32[4,4,256]{2,1,0:T(4,128)S(1)}, /*index=5*/f32[4,256,4]{1,...) conditional(s32[]{:T(128)} %bitcast.124, (bf16[512,512]{1,0:T(8,128)(2,1)}, ...), branch_computations={%region_0.22_spmd, %region_22.60_spmd} | conditional | flops 52090658816 | bytes 669665216
  229.8 3.1 reshape.595
  232.9 2.7 copy.220
  242.0 4.6 convolution_add_fusion.9
  250.1 3.1 fusion.202
  258.6 2.3 fusion.203
  261.1 3.3 fusion.204
  267.8 18.9 %convolution_add_fusion.8 = f32[256,4096]{1,0:T(8,128)S(1)} fusion(bf16[1024,4096]{1,0:T(8,128)(2,1)} %get-tuple-element.460, f32[4096]{0:T(1024)S(1)} %slice.268, f32[256,1024]{1,0:T(8,128)S(1)} %get-tuple-element.858, f32[1024]{0:T(1024)S(1)} %add.416, f32[1024]{0:T(1024)S(1)} %mul.448, f32[256]{0:T(256)S(1)} %fusion.263, ...), kind=kOutput, calls=%fused_computation.302 | convolution fusion | flops 2149842944 | bytes 13658112 | tf_op jit(solution)/shard_map/cond/branch_0_fun/dot_general | solution.py:48
  286.8 8.0 %fusion.297 = (f32[256]{0:T(256)S(1)}, f32[256,1024]{1,0:T(8,128)S(1)}) fusion(f32[1024]{0:T(1024)S(1)} %copy-done.117, f32[256,1024]{1,0:T(8,128)} %copy-done.17, bf16[4096,1024]{1,0:T(8,128)(2,1)} %get-tuple-element.461, f32[256,4096]{1,0:T(8,128)S(1)} %convolution_add_fusion.8), kind=kOutput, calls=%fused_computation.513 | convolution fusion | flops 2157707008 | bytes 14685184 | tf_op jit(solution)/shard_map/cond/branch_0_fun/dot_general | solution.py:48
  299.4 2.3 add_convert_fusion.12.own
  301.7 3.7 copy.252.tab_a
  305.5 231.3 %head.1 = (bf16[1024,256]{1,0:T(8,128)(2,1)}, f32[1,256]{1,0:T(1,128)}) custom-call(bf16[256,1024]{1,0:T(8,128)(2,1)} %add_convert_fusion.12.own, bf16[1664,1024]{1,0:T(8,128)(2,1)} %copy.252.tab_a, bf16[1024,1664]{1,0:T(8,128)(2,1)} %copy-done.4, bf16[1664,1024]{1,0:T(8,128)(2,1)} %get-tuple-element.464.tab_b, bf16[1024,1664]{1,0:T(8,128)(2,1)} %get-tuple-element.465.turn_b), custom_call_target="tpu_custom_call" | custom-call | tf_op jit(solution)/shard_map/cond/branch_0_fun/head/pallas_call | solution.py:1091
  538.3 2.4 multiply_reduce_fusion.11
  540.7 2.7 fusion.286
  543.5 11.6 %multiply_reduce_fusion.10 = (f32[256]{0:T(256)S(1)}, f32[256,1024]{1,0:T(8,128)S(1)}) fusion(f32[256,1024]{1,0:T(8,128)S(1)} %copy-done.18, f32[256]{0:T(256)S(1)} %copy-done.96, f32[1024]{0:T(1024)S(1)} %copy-done.110, bf16[1024,4096]{1,0:T(8,128)(2,1)} %get-tuple-element.460, f32[256,4096]{1,0:T(8,128)} %copy-done.120, ...), kind=kOutput, calls=%fused_computation.380 | convolution fusion | flops 4317511680 | bytes 24124416 | tf_op jit(solution)/shard_map/cond/branch_0_fun/dot_general | solution.py:52
  559.8 3.4 multiply_reduce_fusion.8
  570.1 2.6 fusion.200
  575.8 3.9 fusion.196
  597.1 29.2 %update.1 = (f32[32,256]{1,0:T(8,128)}, f32[32,256]{1,0:T(8,128)}, f32[1,128]{1,0:T(1,128)}) custom-call(f32[32,1,1152]{2,1,0:T(1,128)} %broadcast_in_dim.128.grads, f32[32,1024]{1,0:T(8,128)} %reshape.605.momenta, f32[32,1024]{1,0:T(8,128)} %reshape.606.weights), custom_call_target="tpu_custom_call" | custom-call | tf_op jit(solution)/shard_map/cond/branch_0_fun/update/pallas_call | solution.py:1188
  (235 shorter events, 78.6 us)
Async XLA Ops:
  23.5 200.7 %copy-start.43 = (f32[4,4,1024]{2,1,0:T(4,128)S(1)}, f32[4,4,1024]{2,1,0:T(4,128)}, u32[]{:S(2)}) copy-start(f32[4,4,1024]{2,1,0:T(4,128)} %param.43) | copy-start | bytes 196612
  23.5 200.7 %copy-start.46 = (f32[4,1024,4]{1,2,0:T(4,128)S(1)}, f32[4,1024,4]{1,2,0:T(4,128)}, u32[]{:S(2)}) copy-start(f32[4,1024,4]{1,2,0:T(4,128)} %param.42) | copy-start | bytes 196612
  241.0 17.1 %copy-start.8 = (bf16[256,1024]{1,0:T(8,128)(2,1)}, bf16[256,1024]{1,0:T(8,128)(2,1)S(1)}, u32[]{:S(2)}) copy-start(bf16[256,1024]{1,0:T(8,128)(2,1)S(1)} %add_convert_fusion.14) | copy-start | bytes 1572868
  266.1 20.7 %copy-start.75 = (f32[256,4]{0,1:T(4,128)}, f32[256,4]{0,1:T(4,128)S(1)}, u32[]{:S(2)}) copy-start(f32[256,4]{0,1:T(4,128)S(1)} %fusion.236) | copy-start | bytes 12292
  267.3 19.4 %copy-start.17 = (f32[256,1024]{1,0:T(8,128)}, f32[256,1024]{1,0:T(8,128)S(1)}, u32[]{:S(2)}) copy-start(f32[256,1024]{1,0:T(8,128)S(1)} %get-tuple-element.858) | copy-start | bytes 3145732
  267.4 19.4 %copy-start.95 = (f32[256]{0:T(256)}, f32[256]{0:T(256)S(1)}, u32[]{:S(2)}) copy-start(f32[256]{0:T(256)S(1)} %broadcast_multiply_fusion.5) | copy-start | bytes 3076
  267.6 19.2 %copy-start.101 = (f32[256]{0:T(256)}, f32[256]{0:T(256)S(1)}, u32[]{:S(2)}) copy-start(f32[256]{0:T(256)S(1)} %multiply_reduce_fusion.13) | copy-start | bytes 3076
  267.7 19.1 %copy-start.107 = (f32[256]{0:T(256)}, f32[256]{0:T(256)S(1)}, u32[]{:S(2)}) copy-start(f32[256]{0:T(256)S(1)} %fusion.263) | copy-start | bytes 3076
  267.7 19.1 %copy-start.109 = (f32[1024]{0:T(1024)}, f32[1024]{0:T(1024)S(1)}, u32[]{:S(2)}) copy-start(f32[1024]{0:T(1024)S(1)} %mul.448) | copy-start | bytes 12292
  267.8 19.0 %copy-start.117 = (f32[1024]{0:T(1024)S(1)}, f32[1024]{0:T(1024)}, u32[]{:S(2)}) copy-start(f32[1024]{0:T(1024)} %get-tuple-element.846) | copy-start | bytes 12292
  286.8 14.9 %copy-start.5 = (bf16[1664,1024]{0,1:T(8,128)(2,1)S(1)}, bf16[1664,1024]{0,1:T(8,128)(2,1)}, u32[]{:S(2)}) copy-start(bf16[1664,1024]{0,1:T(8,128)(2,1)} %get-tuple-element.738) | copy-start | bytes 10223620
  305.4 232.8 %copy-start.86 = (s32[256]{0:T(256)S(1)}, s32[256]{0:T(256)}, u32[]{:S(2)}) copy-start(s32[256]{0:T(256)} %get-tuple-element.458) | copy-start | bytes 3076
  305.4 232.8 %copy-start.112 = (f32[1,1024]{1,0:T(1,128)S(1)}, f32[1,1024]{1,0:T(1,128)}, u32[]{:S(2)}) copy-start(f32[1,1024]{1,0:T(1,128)} %get-tuple-element.468) | copy-start | bytes 12292
  305.4 232.8 %copy-start.11 = (f32[256,1024]{1,0:T(8,128)S(1)}, f32[256,1024]{1,0:T(8,128)}, u32[]{:S(2)}) copy-start(f32[256,1024]{1,0:T(8,128)} %copy-done.10) | copy-start | bytes 3145732
  305.4 232.8 %copy-start.55 = (f32[1024]{0:T(1024)S(1)}, f32[1024]{0:T(1024)}, u32[]{:S(2)}) copy-start(f32[1024]{0:T(1024)} %mul.458) | copy-start | bytes 12292
  305.4 232.8 %copy-start.76 = (f32[1024]{0:T(1024)S(1)}, f32[1024]{0:T(1024)}, u32[]{:S(2)}) copy-start(f32[1024]{0:T(1024)} %add.427) | copy-start | bytes 12292
  305.4 232.8 %copy-start.80 = (f32[256]{0:T(256)S(1)}, f32[256]{0:T(256)}, u32[]{:S(2)}) copy-start(f32[256]{0:T(256)} %copy-done.79) | copy-start | bytes 3076
  305.5 232.8 %copy-start.81 = (f32[256]{0:T(256)S(1)}, f32[256]{0:T(256)}, u32[]{:S(2)}) copy-start(f32[256]{0:T(256)} %fusion.264) | copy-start | bytes 3076
  305.5 235.2 %copy-start.104 = (f32[256]{0:T(256)S(1)}, f32[256]{0:T(256)}, u32[]{:S(2)}) copy-start(f32[256]{0:T(256)} %copy-done.103) | copy-start | bytes 3076
  543.4 11.7 %copy-start.102 = (f32[256]{0:T(256)S(1)}, f32[256]{0:T(256)}, u32[]{:S(2)}) copy-start(f32[256]{0:T(256)} %copy-done.101) | copy-start | bytes 3076
  543.5 11.7 %copy-start.108 = (f32[256]{0:T(256)S(1)}, f32[256]{0:T(256)}, u32[]{:S(2)}) copy-start(f32[256]{0:T(256)} %copy-done.107) | copy-start | bytes 3076
  543.5 12.1 %copy-start.36 = (f32[256,1024]{1,0:T(8,128)S(1)}, f32[256,1024]{1,0:T(8,128)}, u32[]{:S(2)}) copy-start(f32[256,1024]{1,0:T(8,128)} %get-tuple-element.827) | copy-start | bytes 3145732
  579.7 15.8 %copy-start.49 = (f32[4,1024,4]{1,2,0:T(4,128)S(1)}, f32[4,1024,4]{1,2,0:T(4,128)}, u32[]{:S(2)}) copy-start(f32[4,1024,4]{1,2,0:T(4,128)} %get-tuple-element.470) | copy-start | bytes 196612
  579.7 15.8 %copy-start.51 = (f32[4,4,1024]{2,1,0:T(4,128)S(1)}, f32[4,4,1024]{2,1,0:T(4,128)}, u32[]{:S(2)}) copy-start(f32[4,4,1024]{2,1,0:T(4,128)} %get-tuple-element.471) | copy-start | bytes 196612
  (36 other events, 164.3 us)

commit v2 on v1

--- a/solution.py
+++ b/solution.py
@@ -468,6 +468,25 @@
     return dp, z, y, x, core, place, along
 
 
+def inner(z):
+    return (z + 1) // 2 % 2
+
+
+def mirror(z, other):
+    return (z // 2 + other // 2) % 2 * 2 + (z + other) % 2
+
+
+def nearness(z, other):
+    k = mirror(z, other)
+    return k + inner(z) * (k // 2) * (5 - 2 * k)
+
+
+def by_nearness(z):
+    far = z // 2 * 3
+    near = 2 - z // 2
+    return (z, z // 2 * 2 + 1 - z % 2, near, 3 - far)
+
+
 def meet_all(devices, group):
     me = lax.axis_index("dp") * group + lax.axis_index("vocab")
     barrier = pltpu.get_barrier_semaphore()
@@ -526,324 +545,6 @@
         lax.fori_loop(1, devices, one, 0)
 
     return start, arrive, sent
-
-
-def gather_kernel(row_counts, table_rows, devices, group, *refs):
-    count = len(row_counts)
-    token_row, token_col, table, table_turned = refs[:4]
-    ins = refs[4 : 4 + count]
-    refs = refs[4 + count :]
-    embedded, target_rows, table_sum, flags, table_other, turned_other = refs[:6]
-    outs = refs[6 : 6 + count]
-    (
-        send_sems,
-        recv_sems,
-        local_sems,
-        table_sems,
-        ask_sems,
-        row_sems,
-        sum_sems,
-        table_here,
-        selector,
-        rows_out,
-        rows_in,
-        ask_out,
-        ask_in,
-        sum_out,
-        sum_in,
-    ) = refs[6 + count :]
-    dp, z, y, x, core, place, along = position()
-    dp_x, dp_y = place(y, 1 - x, core), place(1 - y, x, core)
-    dp_core, dp_diagonal = place(y, x, 1 - core), place(1 - y, 1 - x, core)
-    peers = [(dp, along[k]) for k in (1, 2, 3)] + [(dp_x, z), (dp_y, z), (dp_core, z)]
-    load = pltpu.make_async_copy(table, table_here, table_sems.at[0])
-    load.start()
-    me = meet_all(devices, group)
-    mine = me
-    sent, kept, used = [], [], [0] * count
-
-    def piece(which, block):
-        rows = row_counts[which]
-        return outs[which].at[pl.ds(pl.multiple_of(block * rows, rows), rows)]
-
-    def send(which, block, peer, source=None):
-        copy = pltpu.make_async_remote_copy(
-            piece(which, block) if source is None else source,
-            piece(which, block),
-            send_sems.at[which, used[which]],
-            recv_sems.at[which, block],
-            device_id=peer,
-            device_id_type=MESH,
-        )
-        used[which] += 1
-        copy.start()
-        sent.append(copy)
-
-    def arrive(which, block):
-        pltpu.make_async_remote_copy(
-            ins[which],
-            piece(which, block),
-            send_sems.at[which, 0],
-            recv_sems.at[which, block],
-            device_id=peers[0],
-            device_id_type=MESH,
-        ).wait_recv()
-
-    def own(which):
-        for peer in peers:
-            send(which, mine, peer, ins[which])
-        copy = pltpu.make_async_copy(ins[which], piece(which, mine), local_sems.at[which])
-        copy.start()
-        kept.append(copy)
-
-    def line(which):
-        for k in (1, 2, 3):
-            block = dp * 4 + along[k]
-            arrive(which, block)
-            for peer in (dp_x, dp_y, dp_core):
-                send(which, block, (peer, z))
-
-    def side(which):
-        for k in range(4):
-            block_x, block_y = dp_x * 4 + along[k], dp_y * 4 + along[k]
-            arrive(which, block_y)
-            if k < 2:
-                send(which, block_y, (dp_x, z))
-            arrive(which, block_x)
-            if k >= 2:
-                send(which, block_x, (dp_y, z))
-            send(which, block_y, (dp_core, z))
-            send(which, block_x, (dp_core, z))
-
-    def diagonal(which):
-        for k in range(4):
-            block = dp_diagonal * 4 + along[k]
-            arrive(which, block)
-            send(which, block, (dp_core, z))
-
-    def other_core(which):
-        for y_at in range(2):
-            for x_at in range(2):
-                for z_at in range(4):
-                    arrive(which, place(y_at, x_at, 1 - core) * 4 + z_at)
-
-    own(0)
-    own(1)
-
-    tokens = token_row.shape[1]
-    wide = (tokens, tokens)
-    ids_row, ids_col = token_row[...], token_col[...]
-    across = lax.broadcasted_iota(jnp.int32, wide, 1).astype(jnp.float32)
-    down = lax.broadcasted_iota(jnp.int32, wide, 0).astype(jnp.float32)
-    owner_row, owner_col = jnp.zeros_like(ids_row), jnp.zeros_like(ids_col)
-    for device in range(1, devices):
-        owner_row += (ids_row >= float(device * table_rows)).astype(jnp.float32)
-        owner_col += (ids_col >= float(device * table_rows)).astype(jnp.float32)
-    equal = ids_col == ids_row
-    first_col = jnp.min(jnp.where(equal, across, float(tokens)), axis=1, keepdims=True)
-    first_row = jnp.min(jnp.where(equal, down, float(tokens)), axis=0, keepdims=True)
-    leads = jnp.where(first_row == across[:1], owner_row, -1.0)
-    slot_col = jnp.sum(
-        jnp.where((owner_col == leads) & (across < first_col), 1.0, 0.0), axis=1, keepdims=True
-    )
-    takes = lax.broadcasted_iota(jnp.int32, (devices, tokens), 0).astype(jnp.float32) == leads
-    local_row = jnp.where(takes, ids_row - owner_row * table_rows + 1.0, 0.0)
-    lanes = lax.broadcasted_iota(jnp.int32, (tokens, 128), 1).astype(jnp.float32)
-    asked = (
-        dot_without_transpose(
-            local_row, (slot_col == lanes).astype(jnp.float32), highest_precision
-        )
-        - 1.0
-    )
-    over = jnp.max(slot_col, axis=0, keepdims=True) >= float(CAP)
-    ask_lanes = lax.broadcasted_iota(jnp.int32, (devices, 128), 1)
-    asked = jnp.where(ask_lanes == 127, over.astype(jnp.float32), asked)
-    ask_out[...] = asked.reshape(devices, 1, 128)
-    ask_in[pl.ds(me, 1)] = ask_out[pl.ds(me, 1)]
-    start, ask_arrive, ask_sent = to_all(
-        lambda other: ask_out.at[other], ask_in, ask_sems.at[0], ask_sems.at[1], devices, group, me
-    )
-    start()
-    load.wait()
-
-    def add_up(step, total):
-        return total + jnp.sum(
-            table_here[pl.ds(pl.multiple_of(step * 128, 128), 128)].astype(jnp.float32),
-            axis=0,
-            keepdims=True,
-        )
-
-    own_sum = lax.fori_loop(
-        0, table_here.shape[0] // 128, add_up, jnp.zeros((1, table_here.shape[1]), jnp.float32)
-    )
-    sum_out[...] = own_sum
-    sum_in[pl.ds(me, 1)] = own_sum[None]
-    start, sum_arrive, sum_sent = to_all(
-        lambda other: sum_out, sum_in, sum_sems.at[0], sum_sems.at[1], devices, group, me
-    )
-    start()
-    ask_arrive()
-    asked_all = ask_in[...].reshape(devices, 128)
-    flags[...] = jnp.broadcast_to(
-        jnp.max(jnp.where(ask_lanes == 127, asked_all, 0.0), axis=0, keepdims=True).max(
-            axis=1, keepdims=True
-        ),
-        flags.shape,
-    )
-    square = (128, 128)
-    eye = (
-        lax.broadcasted_iota(jnp.int32, square, 0) == lax.broadcasted_iota(jnp.int32, square, 1)
-    ).astype(jnp.float32)
-    turned = dot_nt(eye, asked_all, highest_precision)
-    turned = jnp.round(turned)
-    row_lanes = lax.broadcasted_iota(jnp.int32, (CAP, table_here.shape[0]), 1).astype(jnp.float32)
-    for source in range(devices):
-        hot = turned[:CAP, source : source + 1] == row_lanes
-        selector[source * CAP : (source + 1) * CAP] = hot.astype(jnp.float32).astype(jnp.bfloat16)
-
-    def pick(step, state):
-        batch = 8 * CAP
-        picked = dot_without_transpose(
-            selector[pl.ds(pl.multiple_of(step * batch, batch), batch)], table_here[...]
-        )
-        rows_out[pl.ds(step * 8, 8)] = picked.astype(jnp.bfloat16).reshape(8, CAP, -1)
-        return state
-
-    lax.fori_loop(0, devices // 8, pick, 0)
-    rows_in[pl.ds(me, 1)] = rows_out[pl.ds(me, 1)]
-    start, rows_arrive, rows_sent = to_all(
-        lambda other: rows_out.at[other],
-        rows_in,
-        row_sems.at[0],
-        row_sems.at[1],
-        devices,
-        group,
-        me,
-    )
-    start()
-
-    line(0)
-    own(2)
-    line(1)
-    side(0)
-    own(3)
-    line(2)
-    side(1)
-    diagonal(0)
-    own(4)
-    line(3)
-    side(2)
-    diagonal(1)
-    swaps = []
-    for at, (here, there) in enumerate(((table, table_other), (table_turned, turned_other))):
-        copy = pltpu.make_async_remote_copy(
-            here,
-            there,
-            table_sems.at[1 + 2 * at],
-            table_sems.at[2 + 2 * at],
-            device_id=(dp_core, z),
-            device_id_type=MESH,
-        )
-        copy.start()
-        swaps.append(copy)
-
-    rows_arrive()
-    index_col = owner_col * CAP + slot_col
-    slots = lax.broadcasted_iota(jnp.int32, (tokens, devices * CAP), 1).astype(jnp.float32)
-    chosen = (index_col == slots).astype(jnp.float32).astype(jnp.bfloat16)
-    taken = dot_without_transpose(chosen, rows_in[...].reshape(devices * CAP, -1))
-    embedded[...] = taken[: tokens // 2]
-    target_rows[...] = taken[tokens // 2 :]
-    sum_arrive()
-    table_sum[...] = jnp.sum(sum_in[...], axis=0)
-
-    line(4)
-    side(3)
-    diagonal(2)
-    side(4)
-    diagonal(3)
-    diagonal(4)
-    for which in range(count):
-        other_core(which)
-    for copy in swaps:
-        copy.wait()
-    for copy in kept:
-        copy.wait()
-    for copy in sent:
-        copy.wait_send()
-    ask_sent()
-    sum_sent()
-    rows_sent()
-
-
-def gather_all(tokens, table, table_turned, table_rows, arrays):
-    count = len(arrays)
-    group = lax.axis_size("vocab")
-    devices = lax.axis_size("dp") * group
-    width = table.shape[1]
-    own_tokens = tokens.shape[0] // 2
-    anywhere, vmem = pl.BlockSpec(memory_space=pl.ANY), pl.BlockSpec(memory_space=pltpu.VMEM)
-    dma = pltpu.SemaphoreType.DMA
-    return pl.pallas_call(
-        partial(gather_kernel, [a.shape[0] for a in arrays], table_rows, devices, group),
-        out_shape=[
-            jax.ShapeDtypeStruct((own_tokens, width), jnp.float32),
-            jax.ShapeDtypeStruct((own_tokens, width), jnp.float32),
-            jax.ShapeDtypeStruct((1, width), jnp.float32),
-            jax.ShapeDtypeStruct((8, 128), jnp.float32),
-            jax.ShapeDtypeStruct(table.shape, table.dtype),
-            jax.ShapeDtypeStruct(table_turned.shape, table.dtype),
-        ]
-        + [jax.ShapeDtypeStruct((devices * a.shape[0],) + a.shape[1:], a.dtype) for a in arrays],
-        in_specs=[vmem, vmem] + [anywhere] * (2 + count),
-        out_specs=[vmem] * 4 + [anywhere] * (2 + count),
-        scratch_shapes=[
-            dma((count, devices)),
-            dma((count, devices)),
-            dma((count,)),
-            dma((5,)),
-            dma((2, devices)),
-            dma((2, devices)),
-            dma((2, devices)),
-            pltpu.VMEM(table.shape, table.dtype),
-            pltpu.VMEM((devices * CAP, table.shape[0]), jnp.bfloat16),
-            pltpu.VMEM((devices, CAP, width), jnp.bfloat16),
-            pltpu.VMEM((devices, CAP, width), jnp.bfloat16),
-            pltpu.VMEM((devices, 1, 128), jnp.float32),
-            pltpu.VMEM((devices, 1, 128), jnp.float32),
-            pltpu.VMEM((1, width), jnp.float32),
-            pltpu.VMEM((devices, 1, width), jnp.float32),
-        ],
-        name="gather_weights",
-        compiler_params=pltpu.CompilerParams(
-            collective_id=1, has_side_effects=True, vmem_limit_bytes=56 * 2**20
-        ),
-    )(
-        tokens.astype(jnp.float32)[None, :],
-        tokens.astype(jnp.float32)[:, None],
-        table,
-        table_turned,
-        *arrays,
-    )
-
-
-def pack_small(parts):
-    flat = jnp.concatenate([a.reshape(-1) for a in parts])
-    room = -(-flat.shape[0] // 8192) * 8192
-    return jnp.pad(flat, (0, room - flat.shape[0])).reshape(16, -1)
-
-
-def unpack_small(packed, shapes):
-    flat = packed.reshape(-1, 16 * packed.shape[1])
-    out, at = [], 0
-    for shape in shapes:
-        size = 1
-        for n in shape:
-            size *= n
-        piece = flat[:, at : at + size].reshape((-1,) + shape)
-        at += size
-        out.append(jnp.moveaxis(piece, 0, -2).reshape(shape[:-1] + (-1,)))
-    return out
 
 
 def head_kernel(table_rows, chunks, own, tab_a, turn_a, tab_b, turn_b, mean_out, lse_out, *refs):
@@ -864,11 +565,12 @@
         back_send,
         back_recv,
     ) = refs
-    dp, z, y, x, core, place, along = position()
+    dp, z, y, x, core, place, _ = position()
+    along = by_nearness(z)
     pad_rows = tab_a.shape[0]
     width, tile = own.shape[1], own.shape[0]
     dev_x, dev_y = (place(y, 1 - x, core), z), (place(1 - y, x, core), z)
-    dev_z = [None] + [(dp, along[k]) for k in (1, 2, 3)]
+    dev_z = [(dp, along[k]) for k in range(4)]
     peers = [dev_x, dev_y] + dev_z[1:]
     loads = []
     for at, (source, target) in enumerate(
@@ -899,7 +601,26 @@
             device_id_type=MESH,
         )
 
-    gives = [give(0, 4 * k, dev_z[k]) for k in (1, 2, 3)]
+    def give_along(k, upward):
+        there = z + 1 if upward else z - 1
+        return pltpu.make_async_remote_copy(
+            hidden.at[4 * k],
+            hidden.at[4 * nearness(there, along[k])],
+            send_sems.at[16 + k + 3 * (not upward and k == 0)],
+            recv_sems.at[4 * nearness(there, along[k])],
+            device_id=(dp, there),
+            device_id_type=MESH,
+        )
+
+    def pass_along(k, act):
+        @pl.when((along[k] <= z) & (z < 3))
+        def _():
+            act(give_along(k, True))
+
+        @pl.when((along[k] >= z) & (z > 0))
+        def _():
+            act(give_along(k, False))
+
     forwards = {}
     for k in range(4):
         forwards[4 * k] = [give(4 * k, 4 * k + 1, dev_x), give(4 * k, 4 * k + 2, dev_y)]
@@ -907,7 +628,8 @@
             forwards[4 * k + 2] = [give(4 * k + 2, 4 * k + 3, dev_x)]
         else:
             forwards[4 * k + 1] = [give(4 * k + 1, 4 * k + 3, dev_y)]
-    for copy in forwards[0] + gives:
+    pass_along(0, lambda copy: copy.start())
+    for copy in forwards[0]:
         copy.start()
 
     def tile_comes(t, parity):
@@ -918,6 +640,8 @@
             @pl.when(t == at)
             def _(at=at):
                 give(0, at, dev_x).wait_recv()
+                if at % 4 == 0:
+                    pass_along(at // 4, lambda copy: copy.start())
                 for copy in forwards.get(at, []):
                     copy.start()
 
@@ -940,7 +664,7 @@
         backs[4 * k + 1] = back(4 * k + 1, k, dev_x)
         backs[4 * k + 2] = back(4 * k + 2, 4 + k, dev_y)
         if k:
-            backs[4 * k] = back(4 * k, 11 + k, dev_z[k])
+            backs[4 * k] = back(4 * k, 11 + mirror(z, along[k]), dev_z[k])
 
     def back_start(t):
         for copy in backs[t]:
@@ -1075,7 +799,9 @@
     merge(0, [12, 13, 14])
     mean_out[...] = part[0]
     lse_out[...] = part_lse[0]
-    for copies in [gives] + list(forwards.values()) + list(backs.values()):
+    for k in range(4):
+        pass_along(k, lambda copy: copy.wait_send())
+    for copies in list(forwards.values()) + list(backs.values()):
         for copy in copies:
             copy.wait_send()
 
@@ -1108,7 +834,7 @@
             pltpu.VMEM((15, width, tile), jnp.bfloat16),
             pltpu.VMEM((15, 1, tile), jnp.float32),
             dma((5,)),
-            dma((16,)),
+            dma((20,)),
             dma((16,)),
             dma((2, 15)),
             dma((2, 15)),
@@ -1202,8 +928,918 @@
     )(grads, momenta, weights)
 
 
+def halves_of(values):
+    high = values.astype(jnp.bfloat16)
+    return high, (values - high.astype(jnp.float32)).astype(jnp.bfloat16)
+
+
+def stacked_halves(values):
+    return jnp.concatenate(halves_of(values), axis=0)
+
+
+def added_halves(values):
+    rows = values.shape[0] // 2
+    return values[:rows] + values[rows:]
+
+
+def dot_tn(left_side, right_side):
+    return dot_first(left_side, right_side)
+
+
+def normal(values):
+    center = values - jnp.mean(values, axis=-1, keepdims=True)
+    spread = lax.rsqrt(jnp.mean(center * center, axis=-1, keepdims=True) + ln_eps)
+    return center * spread, spread
+
+
+def normal_back(values, gain, gradient):
+    unit, spread = normal(values)
+    pulled = gradient * gain
+    along = jnp.mean(pulled * unit, axis=-1, keepdims=True)
+    return spread * (pulled - jnp.mean(pulled, axis=-1, keepdims=True) - unit * along)
+
+
+def sequence_places(lengths, rows):
+    col = lax.broadcasted_iota(jnp.int32, (rows, 1), 0)
+    row = lax.broadcasted_iota(jnp.int32, (1, rows), 1)
+    segment_col, segment_row = jnp.zeros_like(col), jnp.zeros_like(row)
+    start_col = jnp.zeros_like(col)
+    end = 0
+    for at in range(lengths.shape[1]):
+        length = lengths[0, at]
+        end = end + length
+        segment_col += (col >= end).astype(jnp.int32)
+        segment_row += (row >= end).astype(jnp.int32)
+        start_col += jnp.where(col >= end, length, 0)
+    allowed = (segment_col == segment_row) & (row <= col)
+    return col - start_col, allowed
+
+
+def pairs_of(width):
+    return width // (2 * HEAD_DIM)
+
+
+def pair_at(pair):
+    return pl.ds(pl.multiple_of(pair * 2 * HEAD_DIM, 2 * HEAD_DIM), 2 * HEAD_DIM)
+
+
+def head_lanes(rows):
+    return lax.broadcasted_iota(jnp.int32, (rows, 2 * HEAD_DIM), 1) < HEAD_DIM
+
+
+def first_part(embedded, positions, lengths, gains, shifts, x0, h1):
+    rows = x0.shape[0]
+    place_col, allowed = sequence_places(lengths, rows)
+    spots = lax.broadcasted_iota(jnp.int32, (rows, positions.shape[0]), 1)
+    hot = (place_col == spots).astype(jnp.float32).astype(jnp.bfloat16)
+    x0[...] = embedded[...] + dot_without_transpose(hot, positions[...])
+    unit, _ = normal(x0[...])
+    h1[...] = (unit * gains[0:1] + shifts[0:1]).astype(jnp.bfloat16)
+    return allowed
+
+
+def adapter_in(adapters, inputs):
+    return added_halves(dot_nt(stacked_halves(adapters), inputs))
+
+
+def adapter_out(inner, outer):
+    high, low = halves_of(inner)
+    top, rest = halves_of(outer)
+    return adapter_scale * dot_tn(
+        jnp.concatenate([high, high, low], axis=0), jnp.concatenate([top, rest, top], axis=0)
+    )
+
+
+def ranks(which, shape):
+    return lax.broadcasted_iota(jnp.int32, shape, 0) // 4 == which
+
+
+def project_part(h1, weight, bias, adapters, inner, joined):
+    width = h1.shape[1]
+    step = 512
+    half = adapters.shape[0] // 2
+    inner[...] = adapter_in(adapters[:half], h1[...])
+    for which in range(3):
+
+        def columns(at, state):
+            here = pl.ds(pl.multiple_of(at * step, step), step)
+            there = pl.ds(pl.multiple_of(which * width + at * step, step), step)
+            outer = jnp.where(ranks(which, (half, step)), adapters[half:, here], 0.0)
+            joined[:, there] = (
+                dot_without_transpose(h1[...], weight[:, there])
+                + bias[:, there]
+                + adapter_out(inner[...], outer)
+            ).astype(jnp.bfloat16)
+            return state
+
+        lax.fori_loop(0, width // step, columns, 0)
+
+
+def attend_part(joined, allowed, probs, mixed):
+    rows, width = mixed.shape
+    lanes = head_lanes(rows)
+
+    def pair_step(pair, state):
+        query = joined[:, pair_at(pair)]
+        keys = joined[:, pair_at(pairs_of(width) + pair)]
+        values = joined[:, pair_at(2 * pairs_of(width) + pair)]
+        outs = []
+        for side in range(2):
+            mine = lanes if side == 0 else ~lanes
+            scores = dot_nt(jnp.where(mine, query, jnp.zeros_like(query)), keys) * score_scale
+            scores = jnp.where(allowed, scores, masked_value)
+            expo = jnp.exp(scores - jnp.max(scores, axis=-1, keepdims=True))
+            chances = (expo / jnp.sum(expo, axis=-1, keepdims=True)).astype(jnp.bfloat16)
+            probs[2 * pair + side] = chances
+            outs.append(dot_without_transpose(chances, values))
+        mixed[:, pair_at(pair)] = jnp.where(lanes, outs[0], outs[1]).astype(jnp.bfloat16)
+        return state
+
+    lax.fori_loop(0, pairs_of(width), pair_step, 0)
+
+
+def output_part(x0, mixed, weight, bias, adapters, inner, gains, shifts, x1, h2):
+    half = adapters.shape[0] // 2
+    width = mixed.shape[1]
+    here = ranks(3, inner.shape)
+    fresh = adapter_in(adapters[:half], mixed[...])
+    inner[...] = jnp.where(here, fresh, inner[...])
+    outer = jnp.where(ranks(3, (half, width)), adapters[half:], 0.0)
+    x1[...] = (
+        x0[...]
+        + dot_without_transpose(mixed[...], weight[...])
+        + bias[:, 3 * width : 4 * width]
+        + adapter_out(inner[...], outer)
+    )
+    unit, _ = normal(x1[...])
+    h2[...] = (unit * gains[1:2] + shifts[1:2]).astype(jnp.bfloat16)
+
+
+def up_part(h2, weight, bias, active, slope):
+    width = h2.shape[1]
+    step = 512
+
+    def columns(at, state):
+        here = pl.ds(pl.multiple_of(at * step, step), step)
+        there = pl.ds(pl.multiple_of(4 * width + at * step, step), step)
+        z = dot_without_transpose(h2[...], weight[:, here]) + bias[:, there]
+        root = 0.7978845608028654
+        square = z * z
+        tanh = jnp.tanh(root * z * (1.0 + 0.044715 * square))
+        half = 0.5 * (1.0 + tanh)
+        active[:, here] = (z * half).astype(jnp.bfloat16)
+        slope[:, here] = (
+            half + 0.5 * z * (1.0 - tanh * tanh) * (root * (1.0 + 3 * 0.044715 * square))
+        ).astype(jnp.bfloat16)
+        return state
+
+    lax.fori_loop(0, weight.shape[1] // step, columns, 0)
+
+
+def down_part(x1, active, weight, bias, gains, shifts, x2, final):
+    hidden, width = weight.shape
+    step = 256
+
+    def columns(at, state):
+        here = pl.ds(pl.multiple_of(at * step, step), step)
+        there = pl.ds(pl.multiple_of(4 * width + hidden + at * step, step), step)
+        x2[:, here] = (
+            x1[:, here]
+            + dot_without_transpose(active[...], weight[:, here])
+            + bias[:, there]
+        )
+        return state
+
+    lax.fori_loop(0, width // step, columns, 0)
+    unit, _ = normal(x2[...])
+    final[...] = (unit * gains[2:3] + shifts[2:3]).astype(jnp.bfloat16)
+
+
+def turn_rows(source, target):
+    width = source.shape[0]
+
+    def rows(at, state):
+        here = pl.ds(pl.multiple_of(at * 128, 128), 128)
+        target[:, here] = source[here].astype(jnp.float32).T.astype(target.dtype)
+        return state
+
+    lax.fori_loop(0, width // 128, rows, 0)
+
+
+def backward_kernel(
+    mean_rows,
+    log_total,
+    mask_row,
+    mask_col,
+    target_rows,
+    table_sum,
+    gains,
+    adapters,
+    final,
+    h1,
+    joined,
+    probs,
+    mixed,
+    inner,
+    x1,
+    slope,
+    x2,
+    w_out,
+    w_up,
+    w_down,
+    grads,
+    numbers,
+    work,
+    dx2,
+    da,
+    dz,
+    dmix,
+    pulls,
+    out_here,
+    up_here,
+    down_here,
+    sems,
+):
+    loads = []
+    for at, (source, target) in enumerate(
+        ((w_down, down_here), (w_up, up_here), (w_out, out_here))
+    ):
+        copy = pltpu.make_async_copy(source, target, sems.at[at])
+        copy.start()
+        loads.append(copy)
+    rows, width = x1.shape
+    half = adapters.shape[0] // 2
+    hidden = slope.shape[1]
+    turn_rows(mean_rows, work)
+    pulled = (1.0 - smooth) * target_rows[...] + (smooth / V) * table_sum[...]
+    row_dots = jnp.sum(final[...].astype(jnp.float32) * pulled, axis=1, keepdims=True)
+    loss = jnp.sum(mask_row[...] * log_total[...], axis=1, keepdims=True) - jnp.sum(
+        mask_col[...] * row_dots, axis=0, keepdims=True
+    )
+    counted = jnp.sum(mask_row[...], axis=1, keepdims=True)
+    lanes = lax.broadcasted_iota(jnp.int32, (1, 128), 1)
+    numbers[...] = jnp.where(lanes == 0, loss, jnp.where(lanes == 1, counted, 0.0))
+    dx2[...] = normal_back(x2[...], gains[2:3], mask_col[...] * (work[...] - pulled))
+    da[...] = dx2[...].astype(jnp.bfloat16)
+    loads[0].wait()
+    step = 512
+
+    def hidden_columns(at, state):
+        here = pl.ds(pl.multiple_of(at * step, step), step)
+        dz[:, here] = (
+            dot_nt(da[...], down_here[here]) * slope[:, here].astype(jnp.float32)
+        ).astype(jnp.bfloat16)
+        return state
+
+    lax.fori_loop(0, hidden // step, hidden_columns, 0)
+    loads[1].wait()
+
+    def columns(at, state):
+        here = pl.ds(pl.multiple_of(at * 256, 256), 256)
+        work[:, here] = dot_nt(dz[...], up_here[here])
+        return state
+
+    lax.fori_loop(0, width // 256, columns, 0)
+    dx1 = dx2[...] + normal_back(x1[...], gains[1:2], work[...])
+    da[...] = dx1.astype(jnp.bfloat16)
+    loads[2].wait()
+    upper = stacked_halves(adapters[half:])
+    inner_halves = stacked_halves(inner[...])
+
+    def adapter_grads(which, gradient, inputs):
+        up_grad = adapter_scale * added_halves(dot_without_transpose(inner_halves, gradient))
+        back = adapter_scale * added_halves(dot_nt(upper, gradient))
+        back = jnp.where(ranks(which, back.shape), back, 0.0)
+        down_grad = added_halves(dot_without_transpose(stacked_halves(back), inputs))
+        keep = ranks(which, up_grad.shape)
+        return back, down_grad, jnp.where(keep, up_grad, 0.0)
+
+    back, down_total, up_total = adapter_grads(3, da[...], mixed[...])
+    dmix[...] = (
+        dot_nt(da[...], out_here[...]) + adapter_out(back, adapters[:half]) / adapter_scale
+    ).astype(jnp.bfloat16)
+    lane_mask = head_lanes(rows)
+
+    def pair_step(pair, state):
+        query = joined[:, pair_at(pair)]
+        keys = joined[:, pair_at(pairs_of(width) + pair)]
+        values = joined[:, pair_at(2 * pairs_of(width) + pair)]
+        pull = dmix[:, pair_at(pair)]
+        outs = []
+        for side in range(2):
+            mine = lane_mask if side == 0 else ~lane_mask
+            chances = probs[2 * pair + side]
+            wide = chances.astype(jnp.float32)
+            reach = dot_nt(jnp.where(mine, pull, jnp.zeros_like(pull)), values)
+            slide = wide * (reach - jnp.sum(wide * reach, axis=-1, keepdims=True))
+            slide = slide.astype(jnp.bfloat16)
+            outs.append(
+                (
+                    dot_without_transpose(slide, keys) * score_scale,
+                    dot_tn(slide, query) * score_scale,
+                    dot_tn(chances, pull),
+                )
+            )
+        for which in range(3):
+            both = jnp.where(lane_mask, outs[0][which], outs[1][which])
+            pulls[:, pair_at(which * pairs_of(width) + pair)] = both.astype(jnp.bfloat16)
+        return state
+
+    lax.fori_loop(0, pairs_of(width), pair_step, 0)
+    for which in range(3):
+        _, down_part_grad, up_part_grad = adapter_grads(
+            which, pulls[:, which * width : (which + 1) * width], h1[...]
+        )
+        down_total += down_part_grad
+        up_total += up_part_grad
+    grads[:half] = down_total
+    grads[half:] = up_total
+
+
+def backward(mean_rows, log_total, mask, target_rows, table_sum, gains, adapters, kept, weights):
+    rows = mask.shape[0]
+    width = target_rows.shape[1]
+    hidden = weights[2].shape[0]
+    low, full = jnp.bfloat16, jnp.float32
+    anywhere, vmem = pl.BlockSpec(memory_space=pl.ANY), pl.BlockSpec(memory_space=pltpu.VMEM)
+    shape = jax.ShapeDtypeStruct
+    return pl.pallas_call(
+        backward_kernel,
+        out_shape=[shape(adapters.shape, full), shape((1, 128), full)],
+        in_specs=[vmem] * (8 + len(kept)) + [anywhere] * 3,
+        out_specs=[vmem] * 2,
+        scratch_shapes=[
+            pltpu.VMEM((rows, width), full),
+            pltpu.VMEM((rows, width), full),
+            pltpu.VMEM((rows, width), low),
+            pltpu.VMEM((rows, hidden), low),
+            pltpu.VMEM((rows, width), low),
+            pltpu.VMEM((rows, 3 * width), low),
+        ]
+        + [pltpu.VMEM(w.shape, low) for w in weights]
+        + [pltpu.SemaphoreType.DMA((3,))],
+        name="backward",
+        compiler_params=pltpu.CompilerParams(vmem_limit_bytes=60 * 2**20),
+    )(
+        mean_rows,
+        log_total,
+        mask[None, :],
+        mask[:, None],
+        target_rows,
+        table_sum,
+        gains,
+        adapters,
+        *kept,
+        *weights,
+    )
+
+
 def stack_adapters(down, up):
     return jnp.concatenate([jnp.swapaxes(down, 1, 2), up], axis=0).reshape(-1, up.shape[2])
+
+
+def col_of(row):
+    size = row.shape[1]
+    square = (size, size)
+    same = lax.broadcasted_iota(jnp.int32, square, 0) == lax.broadcasted_iota(jnp.int32, square, 1)
+    return jnp.sum(jnp.where(same, row, 0.0), axis=1, keepdims=True)
+
+
+def stack_rows(down, up):
+    return jnp.concatenate(
+        [down[j] for j in range(down.shape[0])] + [up[j] for j in range(up.shape[0])], axis=0
+    )
+
+
+def pack_rows(positions, gains, shifts, biases):
+    places = positions[...].astype(jnp.float32)
+    span = places.shape[0] // 4
+    width = places.shape[1]
+    places = jnp.concatenate([places[r * span : (r + 1) * span] for r in range(4)], axis=1)
+    norms = jnp.concatenate(
+        [
+            gains[...].astype(jnp.float32),
+            shifts[...].astype(jnp.float32),
+            jnp.zeros((gains.shape[0], 128 - 2 * width), jnp.float32),
+        ],
+        axis=1,
+    )
+    flat = biases[...].astype(jnp.float32)
+    flat = jnp.concatenate([flat, jnp.zeros((1, -flat.shape[1] % 128), jnp.float32)], axis=1)
+    lines = [flat[:, r * 128 : (r + 1) * 128] for r in range(flat.shape[1] // 128)]
+    rest = jnp.zeros((8 - gains.shape[0], 128), jnp.float32)
+    tail = jnp.zeros((8 - len(lines), 128), jnp.float32)
+    return jnp.concatenate([places, norms, rest] + lines + [tail], axis=0).astype(jnp.bfloat16)
+
+
+def unpack_rows(packed, devices, width, span, norms, bias_size, positions, gains, shifts, bias):
+    rows = packed.shape[0] // devices
+
+    def group(j, state):
+        devs = [
+            packed[pl.ds(pl.multiple_of((4 * j + i) * rows, rows), rows)].astype(jnp.float32)
+            for i in range(4)
+        ]
+        lanes = pl.ds(pl.multiple_of(j * 128, 128), 128)
+        for r in range(4):
+            block = [dev[:span, r * width : (r + 1) * width] for dev in devs]
+            positions[r * span : (r + 1) * span, lanes] = jnp.concatenate(block, axis=1).astype(
+                jnp.bfloat16
+            )
+        gains[:, lanes] = jnp.concatenate([dev[span : span + norms, :width] for dev in devs], axis=1)
+        shifts[:, lanes] = jnp.concatenate(
+            [dev[span : span + norms, width : 2 * width] for dev in devs], axis=1
+        )
+        flat = []
+        for dev in devs:
+            left = bias_size
+            line = span + 8
+            while left > 0:
+                flat.append(dev[line : line + 1, : min(left, 128)])
+                left -= 128
+                line += 1
+        bias[:, pl.ds(pl.multiple_of(j * 4 * bias_size, 128), 4 * bias_size)] = jnp.concatenate(
+            flat, axis=1
+        )
+        return state
+
+    lax.fori_loop(0, devices // 4, group, 0)
+
+
+def first_kernel(table_rows, devices, group, row_counts, *refs):
+    (
+        ids,
+        targets,
+        mask,
+        lengths,
+        position_own,
+        gain_own,
+        shift_own,
+        bias_own,
+        adapter_down,
+        adapter_up,
+        table_tail,
+        table,
+        *refs,
+    ) = refs
+    weights_own = refs[:4]
+    refs = refs[4:]
+    (
+        flags,
+        target_out,
+        table_sum,
+        gains_out,
+        adapters_out,
+        final,
+        inner,
+        table_mine,
+        turned_mine,
+        table_other,
+        turned_other,
+        h1_out,
+        joined_out,
+        probs_out,
+        mixed_out,
+        x1_out,
+        slope_out,
+        x2_out,
+        out_kept,
+        up_kept,
+        down_kept,
+        *refs,
+    ) = refs
+    (
+        send_sems,
+        recv_sems,
+        local_sems,
+        table_sems,
+        ask_sems,
+        row_sems,
+        sum_sems,
+        keep_sems,
+        table_here,
+        turned_here,
+        selector,
+        rows_out,
+        rows_in,
+        ask_out,
+        ask_in,
+        sum_out,
+        sum_in,
+        pack_here,
+        packed,
+        w_qkv,
+        w_out,
+        w_up,
+        w_down,
+        positions,
+        shifts,
+        bias,
+        embedded,
+        x0,
+        h1,
+        joined,
+        probs,
+        mixed,
+        x1,
+        h2,
+        active,
+        slope,
+        x2,
+    ) = refs
+    arrays = (packed, w_qkv, w_out, w_up, w_down)
+    ins = (pack_here,) + tuple(weights_own)
+    dp, z, y, x, core, place, along = position()
+    dp_x, dp_y = place(y, 1 - x, core), place(1 - y, x, core)
+    dp_core, dp_diagonal = place(y, x, 1 - core), place(1 - y, 1 - x, core)
+    z_peers = [(dp, along[k]) for k in (1, 2, 3)]
+    near_peers = [(dp_x, z), (dp_y, z), (dp_core, z)]
+    body_rows = table_rows // 16 * 16
+    tail_rows = table_here.shape[0] - body_rows
+    loads = [
+        pltpu.make_async_copy(
+            table.at[pl.ds(0, body_rows)], table_here.at[pl.ds(0, body_rows)], table_sems.at[0]
+        ),
+        pltpu.make_async_copy(
+            table_tail, table_here.at[pl.ds(body_rows, tail_rows)], table_sems.at[1]
+        ),
+    ]
+    for copy in loads:
+        copy.start()
+    pack_here[...] = pack_rows(position_own, gain_own, shift_own, bias_own)
+    me = meet_all(devices, group)
+    sent, kept, used = [], [], [0] * len(arrays)
+
+    def piece(which, block):
+        rows = row_counts[which]
+        return arrays[which].at[pl.ds(pl.multiple_of(block * rows, rows), rows)]
+
+    def send(which, block, peer, source=None):
+        copy = pltpu.make_async_remote_copy(
+            piece(which, block) if source is None else source,
+            piece(which, block),
+            send_sems.at[which, used[which]],
+            recv_sems.at[which, block],
+            device_id=peer,
+            device_id_type=MESH,
+        )
+        used[which] += 1
+        copy.start()
+        sent.append(copy)
+
+    def arrive(which, block):
+        pltpu.make_async_remote_copy(
+            ins[which],
+            piece(which, block),
+            send_sems.at[which, 0],
+            recv_sems.at[which, block],
+            device_id=z_peers[0],
+            device_id_type=MESH,
+        ).wait_recv()
+
+    def own_near(which):
+        for peer in near_peers:
+            send(which, me, peer, ins[which])
+        copy = pltpu.make_async_copy(ins[which], piece(which, me), local_sems.at[which])
+        copy.start()
+        kept.append(copy)
+
+    def own_z(which):
+        for peer in z_peers:
+            send(which, me, peer, ins[which])
+
+    def line(which):
+        for k in (1, 2, 3):
+            block = dp * 4 + along[k]
+            arrive(which, block)
+            for peer in near_peers:
+                send(which, block, peer)
+
+    def side(which):
+        for k in range(4):
+            block_x, block_y = dp_x * 4 + along[k], dp_y * 4 + along[k]
+            arrive(which, block_y)
+            if k < 2:
+                send(which, block_y, (dp_x, z))
+            arrive(which, block_x)
+            if k >= 2:
+                send(which, block_x, (dp_y, z))
+            send(which, block_y, (dp_core, z))
+            send(which, block_x, (dp_core, z))
+
+    def diagonal(which):
+        for k in range(4):
+            block = dp_diagonal * 4 + along[k]
+            arrive(which, block)
+            send(which, block, (dp_core, z))
+
+    def other_core(which):
+        for y_at in range(2):
+            for x_at in range(2):
+                for z_at in range(4):
+                    arrive(which, place(y_at, x_at, 1 - core) * 4 + z_at)
+        kept[which].wait()
+
+    def keep(at, source, target):
+        copy = pltpu.make_async_copy(source, target, keep_sems.at[at])
+        copy.start()
+        return copy
+
+    for which in range(len(arrays)):
+        own_near(which)
+    own_z(0)
+    own_z(1)
+
+    own_ids = ids[...].astype(jnp.float32)
+    own_targets = jnp.where(mask[...] > 0, targets[...], ids[...]).astype(jnp.float32)
+    ids_row = jnp.concatenate([own_ids, own_targets], axis=1)
+    ids_col = jnp.concatenate([col_of(own_ids), col_of(own_targets)], axis=0)
+    tokens = ids_row.shape[1]
+    wide = (tokens, tokens)
+    across = lax.broadcasted_iota(jnp.int32, wide, 1).astype(jnp.float32)
+    down = lax.broadcasted_iota(jnp.int32, wide, 0).astype(jnp.float32)
+    owner_row, owner_col = jnp.zeros_like(ids_row), jnp.zeros_like(ids_col)
+    for device in range(1, devices):
+        owner_row += (ids_row >= float(device * table_rows)).astype(jnp.float32)
+        owner_col += (ids_col >= float(device * table_rows)).astype(jnp.float32)
+    equal = ids_col == ids_row
+    first_col = jnp.min(jnp.where(equal, across, float(tokens)), axis=1, keepdims=True)
+    first_row = jnp.min(jnp.where(equal, down, float(tokens)), axis=0, keepdims=True)
+    leads = jnp.where(first_row == across[:1], owner_row, -1.0)
+    slot_col = jnp.sum(
+        jnp.where((owner_col == leads) & (across < first_col), 1.0, 0.0), axis=1, keepdims=True
+    )
+    takes = lax.broadcasted_iota(jnp.int32, (devices, tokens), 0).astype(jnp.float32) == leads
+    local_row = jnp.where(takes, ids_row - owner_row * table_rows + 1.0, 0.0)
+    lanes = lax.broadcasted_iota(jnp.int32, (tokens, 128), 1).astype(jnp.float32)
+    asked = (
+        dot_without_transpose(
+            local_row, (slot_col == lanes).astype(jnp.float32), highest_precision
+        )
+        - 1.0
+    )
+    over = jnp.max(slot_col, axis=0, keepdims=True) >= float(CAP)
+    ask_lanes = lax.broadcasted_iota(jnp.int32, (devices, 128), 1)
+    asked = jnp.where(ask_lanes == 127, over.astype(jnp.float32), asked)
+    ask_out[...] = asked.reshape(devices, 1, 128)
+    ask_in[pl.ds(me, 1)] = ask_out[pl.ds(me, 1)]
+    start, ask_arrive, ask_sent = to_all(
+        lambda other: ask_out.at[other], ask_in, ask_sems.at[0], ask_sems.at[1], devices, group, me
+    )
+    start()
+    own_z(2)
+    for copy in loads:
+        copy.wait()
+    keeps = [keep(0, table_here, table_mine)]
+
+    def add_up(step, total):
+        return total + jnp.sum(
+            table_here[pl.ds(pl.multiple_of(step * 128, 128), 128)].astype(jnp.float32),
+            axis=0,
+            keepdims=True,
+        )
+
+    own_sum = lax.fori_loop(
+        0, table_here.shape[0] // 128, add_up, jnp.zeros((1, table_here.shape[1]), jnp.float32)
+    )
+    sum_out[...] = own_sum
+    sum_in[pl.ds(me, 1)] = own_sum[None]
+    start, sum_arrive, sum_sent = to_all(
+        lambda other: sum_out, sum_in, sum_sems.at[0], sum_sems.at[1], devices, group, me
+    )
+    start()
+    line(0)
+    line(1)
+    own_z(3)
+    ask_arrive()
+    asked_all = ask_in[...].reshape(devices, 128)
+    flags[...] = jnp.broadcast_to(
+        jnp.max(
+            jnp.max(jnp.where(ask_lanes == 127, asked_all, 0.0), axis=0, keepdims=True),
+            axis=1,
+            keepdims=True,
+        ),
+        flags.shape,
+    )
+    square = (128, 128)
+    eye = (
+        lax.broadcasted_iota(jnp.int32, square, 0) == lax.broadcasted_iota(jnp.int32, square, 1)
+    ).astype(jnp.float32)
+    turned = jnp.round(dot_nt(eye, asked_all, highest_precision))
+    row_lanes = lax.broadcasted_iota(jnp.int32, (CAP, table_here.shape[0]), 1).astype(jnp.float32)
+    batch = 8
+    for step in range(devices // batch):
+        for at in range(batch):
+            source = step * batch + at
+            hot = turned[:CAP, source : source + 1] == row_lanes
+            selector[at * CAP : (at + 1) * CAP] = hot.astype(jnp.float32).astype(jnp.bfloat16)
+        picked = dot_without_transpose(selector[...], table_here[...])
+        rows_out[step * batch : (step + 1) * batch] = picked.astype(jnp.bfloat16).reshape(
+            batch, CAP, -1
+        )
+    rows_in[pl.ds(me, 1)] = rows_out[pl.ds(me, 1)]
+    start, rows_arrive, rows_sent = to_all(
+        lambda other: rows_out.at[other],
+        rows_in,
+        row_sems.at[0],
+        row_sems.at[1],
+        devices,
+        group,
+        me,
+    )
+    start()
+    side(0)
+    line(2)
+    side(1)
+    own_z(4)
+    adapters = adapters_out
+    adapters[...] = stack_rows(adapter_down, adapter_up)
+    turn_rows(table_here, turned_here)
+    keeps.append(keep(1, turned_here, turned_mine))
+    swaps = []
+    for at, (here, there) in enumerate(((table_here, table_other), (turned_here, turned_other))):
+        copy = pltpu.make_async_remote_copy(
+            here,
+            there,
+            table_sems.at[2 + 2 * at],
+            table_sems.at[3 + 2 * at],
+            device_id=(dp_core, z),
+            device_id_type=MESH,
+        )
+        copy.start()
+        swaps.append(copy)
+    diagonal(0)
+    line(3)
+    side(2)
+    other_core(0)
+    unpack_rows(
+        packed,
+        devices,
+        position_own.shape[1],
+        position_own.shape[0] // 4,
+        gain_own.shape[0],
+        bias_own.shape[1],
+        positions,
+        gains_out,
+        shifts,
+        bias,
+    )
+    diagonal(1)
+
+    rows_arrive()
+    index_col = owner_col * CAP + slot_col
+    slots = lax.broadcasted_iota(jnp.int32, (tokens, devices * CAP), 1).astype(jnp.float32)
+    chosen = (index_col == slots).astype(jnp.float32).astype(jnp.bfloat16)
+    taken = dot_without_transpose(chosen, rows_in[...].reshape(devices * CAP, -1))
+    embedded[...] = taken[: tokens // 2]
+    target_out[...] = taken[tokens // 2 :]
+    sum_arrive()
+    table_sum[...] = jnp.sum(sum_in[...], axis=0)
+    allowed = first_part(embedded, positions, lengths, gains_out, shifts, x0, h1)
+    keeps.append(keep(2, h1, h1_out))
+    line(4)
+    side(3)
+    other_core(1)
+    project_part(h1, w_qkv, bias, adapters, inner, joined)
+    keeps.append(keep(3, joined, joined_out))
+    diagonal(2)
+    side(4)
+    attend_part(joined, allowed, probs, mixed)
+    keeps.append(keep(4, probs, probs_out))
+    keeps.append(keep(5, mixed, mixed_out))
+    diagonal(3)
+    other_core(2)
+    keeps.append(keep(6, w_out, out_kept))
+    output_part(x0, mixed, w_out, bias, adapters, inner, gains_out, shifts, x1, h2)
+    keeps.append(keep(7, x1, x1_out))
+    diagonal(4)
+    other_core(3)
+    keeps.append(keep(8, w_up, up_kept))
+    up_part(h2, w_up, bias, active, slope)
+    keeps.append(keep(9, slope, slope_out))
+    other_core(4)
+    keeps.append(keep(10, w_down, down_kept))
+    down_part(x1, active, w_down, bias, gains_out, shifts, x2, final)
+    keeps.append(keep(11, x2, x2_out))
+    for copy in swaps:
+        copy.wait()
+    for copy in keeps:
+        copy.wait()
+    for copy in sent:
+        copy.wait_send()
+    ask_sent()
+    sum_sent()
+    rows_sent()
+
+
+def first(
+    ids, targets, mask, lengths, table, small, adapter_down, adapter_up, weights
+):
+    group = lax.axis_size("vocab")
+    devices = lax.axis_size("dp") * group
+    table_rows, width = table.shape
+    pad_rows = -(-table_rows // 128) * 128
+    body_rows = table_rows // 16 * 16
+    tail = jnp.pad(table[body_rows:], ((0, pad_rows - table_rows), (0, 0)))
+    rows = ids.shape[0]
+    hidden = weights[3].shape[0] * devices
+    heads = width // HEAD_DIM
+    low, full = jnp.bfloat16, jnp.float32
+    positions, gains, shifts, biases = small
+    pack_height = positions.shape[0] // 4 + 16
+    counts = [pack_height] + [w.shape[0] for w in weights]
+    anywhere, vmem = pl.BlockSpec(memory_space=pl.ANY), pl.BlockSpec(memory_space=pltpu.VMEM)
+    dma = pltpu.SemaphoreType.DMA
+    shape = jax.ShapeDtypeStruct
+    adapter_rows = 2 * adapter_up.shape[0] * adapter_up.shape[1]
+    whole = [(devices * w.shape[0], w.shape[1]) for w in weights]
+    saved = [
+        shape((pad_rows, width), low),
+        shape((width, pad_rows), low),
+        shape((pad_rows, width), low),
+        shape((width, pad_rows), low),
+        shape((rows, width), low),
+        shape((rows, 3 * width), low),
+        shape((heads, rows, rows), low),
+        shape((rows, width), low),
+        shape((rows, width), full),
+        shape((rows, hidden), low),
+        shape((rows, width), full),
+    ] + [shape(w, low) for w in whole[1:]]
+    return pl.pallas_call(
+        partial(first_kernel, table_rows, devices, group, counts),
+        out_shape=[
+            shape((8, 128), full),
+            shape((rows, width), full),
+            shape((1, width), full),
+            shape((gains.shape[0], width), full),
+            shape((adapter_rows, width), full),
+            shape((rows, width), low),
+            shape((adapter_rows // 2, rows), full),
+        ]
+        + saved,
+        in_specs=[vmem] * 3
+        + [pl.BlockSpec(memory_space=pltpu.SMEM)]
+        + [vmem] * 6
+        + [anywhere] * (2 + len(weights)),
+        out_specs=[vmem] * 7 + [anywhere] * len(saved),
+        scratch_shapes=[
+            dma((len(counts), devices)),
+            dma((len(counts), devices)),
+            dma((len(counts),)),
+            dma((6,)),
+            dma((2, devices)),
+            dma((2, devices)),
+            dma((2, devices)),
+            dma((12,)),
+            pltpu.VMEM((pad_rows, width), low),
+            pltpu.VMEM((width, pad_rows), low),
+            pltpu.VMEM((8 * CAP, pad_rows), low),
+            pltpu.VMEM((devices, CAP, width), low),
+            pltpu.VMEM((devices, CAP, width), low),
+            pltpu.VMEM((devices, 1, 128), full),
+            pltpu.VMEM((devices, 1, 128), full),
+            pltpu.VMEM((1, width), full),
+            pltpu.VMEM((devices, 1, width), full),
+            pltpu.VMEM((pack_height, 128), low),
+            pltpu.VMEM((devices * pack_height, 128), low),
+        ]
+        + [pltpu.VMEM(w, low) for w in whole]
+        + [
+            pltpu.VMEM((positions.shape[0], width), low),
+            pltpu.VMEM((shifts.shape[0], width), full),
+            pltpu.VMEM((1, devices * biases.shape[0]), full),
+            pltpu.VMEM((rows, width), full),
+            pltpu.VMEM((rows, width), full),
+            pltpu.VMEM((rows, width), low),
+            pltpu.VMEM((rows, 3 * width), low),
+            pltpu.VMEM((heads, rows, rows), low),
+            pltpu.VMEM((rows, width), low),
+            pltpu.VMEM((rows, width), full),
+            pltpu.VMEM((rows, width), low),
+            pltpu.VMEM((rows, hidden), low),
+            pltpu.VMEM((rows, hidden), low),
+            pltpu.VMEM((rows, width), full),
+        ],
+        name="first",
+        compiler_params=pltpu.CompilerParams(
+            collective_id=1, has_side_effects=True, vmem_limit_bytes=63 * 2**20
+        ),
+    )(
+        ids[None, :],
+        targets[None, :],
+        mask[None, :],
+        lengths,
+        positions,
+        gains,
+        shifts,
+        biases[None, :],
+        jnp.swapaxes(adapter_down, 1, 2),
+        adapter_up,
+        tail,
+        table,
+        *weights,
+    )
 
 
 def per_device(
@@ -1245,74 +1881,63 @@
         up_momentum,
     )
     table_rows = table.shape[0]
-    row_count = ids.shape[0]
-    table = jnp.pad(table, ((0, -table_rows % 128), (0, 0)))
-    table_turned = table.T
-    tokens = jnp.concatenate([ids, jnp.where(counted_mask > 0, targets, ids)])
-    small = (position_table, layer_norm_gain, layer_norm_bias, biases)
     (
-        embedded,
+        flags,
         target_rows,
         table_sum,
-        flags,
+        gains_all,
+        adapters,
+        final_state,
+        inner_rows,
+        table_mine,
+        turned_mine,
         table_other,
         turned_other,
-        packed,
-        w_qkv_all,
+        h1,
+        joined,
+        probs,
+        mixed,
+        x1,
+        slope,
+        x2,
         w_out_all,
         w_up_all,
         w_down_all,
-    ) = gather_all(
-        tokens,
+    ) = first(
+        ids,
+        targets,
+        counted_mask,
+        lengths,
         table,
-        table_turned,
-        table_rows,
-        (pack_small(small), query_key_value_weight, output_weight, up_weight, down_weight),
-    )
+        (position_table, layer_norm_gain, layer_norm_bias, biases),
+        adapter_down,
+        adapter_up,
+        (query_key_value_weight, output_weight, up_weight, down_weight),
+    )
+    kept = (h1, joined, probs, mixed, inner_rows, x1, slope, x2)
 
     def go_on():
-        positions_all, gains_all, shifts_all, bias_stack = unpack_small(
-            packed, [a.shape for a in small]
-        )
-        positions_in, allowed_mask = layout(lengths[0], row_count)
-        residual_initial = embedded + positions_all[positions_in].astype(jnp.float32)
-        frozen_weights = (
-            w_qkv_all,
-            w_out_all,
-            w_up_all,
-            w_down_all,
+        mean_rows, log_total = head(
+            final_state, table_rows, (table_mine, turned_mine, table_other, turned_other)
+        )
+        grads, sums = backward(
+            mean_rows,
+            log_total,
+            counted_mask.astype(jnp.float32),
+            target_rows,
+            table_sum,
             gains_all,
-            shifts_all,
-            bias_stack,
-        )
-        final_state, kept_rows = layer_forward(
-            residual_initial, frozen_weights, adapter_down, adapter_up, allowed_mask
-        )
-        mean_rows, log_total = head(
-            final_state, table_rows, (table, table_turned, table_other, turned_other)
-        )
-        mean_rows = mean_rows.T.astype(jnp.float32)
-        log_total = log_total[0]
-        state_float = final_state.astype(jnp.float32)
-        uniform = (smooth / V) * table_sum
-        pulled = (1.0 - smooth) * target_rows + uniform
-        row_loss = log_total - jnp.sum(state_float * pulled, axis=1)
-        mask_float = counted_mask.astype(jnp.float32)
-        loss_own = jnp.sum(mask_float * row_loss)
-        count_own = jnp.sum(mask_float)
-        final_gradient = mask_float[:, None] * (mean_rows - pulled)
-        backward_weights = (w_out_all, w_up_all, w_down_all, gains_all)
-        down_gradient, up_gradient = layer_backward(
-            final_gradient, kept_rows, backward_weights, adapter_down, adapter_up, allowed_mask
-        )
-        grads = stack_adapters(down_gradient, up_gradient)
-        extra = jnp.zeros((grads.shape[0], 128), jnp.float32)
-        extra = extra.at[:, 0].set(loss_own).at[:, 1].set(count_own)
-        grads = jnp.concatenate([grads, extra], axis=1)[:, None, :]
+            adapters,
+            (final_state, *kept),
+            (w_out_all, w_up_all, w_down_all),
+        )
+        grads = jnp.concatenate(
+            [grads, jnp.broadcast_to(sums, (grads.shape[0], sums.shape[1]))], axis=1
+        )[:, None, :]
         new_momenta, new_weights, numbers = update(
             grads,
             stack_adapters(down_momentum, up_momentum),
-            stack_adapters(adapter_down, adapter_up),
+            adapters,
         )
 
         def split(stacked):

time: 653 us -> 506 us (0.77)
  matrix products: 83.3 us -> 0 us
  local copies, waits for them, and re-layouts: 71.1 us -> 13.2 us
  other arithmetic: 21.5 us -> 2.16 us
  Pallas kernels: 446 us -> 457 us
    dot_general x33 -> x0, matrix products: 83.3 us -> none  [the longest x12 41.8 us: dot_without_transpose(): jnp.dot(left_side, right_side, precision=setting, preferred_element_type=...]
    pallas_call x1 -> x2, Pallas kernels: 185 us -> 200 us  [the longest x1 175 us: first(): pl.pallas_call(partial(first_kernel, table_rows, devices, group, counts),...]
    reshape x7 -> x0, local copies, waits for them, and re-layouts: 11.8 us -> none  [the longest x3 4.04 us: pack_small(): flat = jnp.concatenate([a.reshape(-1) for a in parts])]
    unnamed x124 -> x27, local copies, waits for them, and re-layouts: 13.6 us -> 2.94 us
    reduce_sum x11 -> x0, other arithmetic: 8.51 us -> none  [the longest x3 3.25 us: layer_norm(): center = values - jnp.mean(values, axis=-1, keepdims=True)]
    convert_element_type x9 -> x1, other arithmetic: 7.38 us -> 0.01 us  [go_on(): counted_mask.astype(jnp.float32)]
    pallas_call x1, Pallas kernels: 29.2 us -> 22.4 us  [update(): pl.pallas_call(partial(update_kernel, devices, group), out_shape=[small,...]
    transpose x2 -> x0, local copies, waits for them, and re-layouts: 6.86 us -> none  [the longest x1 4.15 us: per_device(): table_turned = table.T]
where the time goes in v2:
time: 506 us; the launch traced here: 497 us
  Pallas kernels  457 us (90%)
  between operations  15.1 us (3%)
  local copies, waits for them, and re-layouts  13.2 us (3%)
  loops' own time  9.86 us (2%)
    pallas_call x1, Pallas kernels, head(): pl.pallas_call(partial(head_kernel, table_rows, chunks), out_shape=[jax.S...  234 us
    pallas_call x1, Pallas kernels, first(): pl.pallas_call(partial(first_kernel, table_rows, devices, group, counts),...  175 us
    pallas_call x1, Pallas kernels, backward(): pl.pallas_call(backward_kernel, out_shape=[shape(adapters.shape, full), s...  25.5 us
    pallas_call x1, Pallas kernels, update(): pl.pallas_call(partial(update_kernel, devices, group), out_shape=[small,...  22.4 us

profile of v2, /device:TPU:0, one launch (start us, length us, event | category | flops | bytes accessed | tf_op | source)
XLA Modules:
  0.0 497.2 jit_solution(9466096599804106089)
XLA Ops:
  7.2 0.0 copy-start.38
  7.3 0.8 slice.111
  8.1 0.7 pad.4.refs_10_
  8.8 1.4 copy.148.refs_4_
  10.2 1.2 broadcast_in_dim.158.refs_7_
  11.5 174.6 %first.1 = (f32[8,128]{1,0:T(8,128)}, f32[256,1024]{1,0:T(8,128)}, f32[1,1024]{1,0:T(1,128)S(1)}, f32[3,1024]{1,0:T(4,128)S(1)}, f32[32,1024]{1,0:T(8,128)S(1)},...) custom-call(s32[1,256]{1,0:T(1,128)} %bitcast.343, ...), custom_call_target="tpu_custom_call" | custom-call | tf_op jit(solution)/shard_map/first/pallas_call | solution.py:1769
  186.0 1.2 slice.112
  188.0 300.9 %conditional.4 = (f32[]{:T(128)}, f32[]{:T(128)}, f32[]{:T(128)}, f32[4,256,4]{1,2,0:T(4,128)S(1)}, f32[4,4,256]{2,1,0:T(4,128)S(1)}, /*index=5*/f32[4,256,4]{1,...) conditional(s32[]{:T(128)} %bitcast.81, (bf16[256,1024]{1,0:T(8,128)(2,1)S(1)}, ...), branch_computations={%region_0.1_spmd, %region_1.39_spmd} | conditional | flops 52090658816 | bytes 670187328
  188.0 234.5 %head.1 = (bf16[1024,256]{1,0:T(8,128)(2,1)}, f32[1,256]{1,0:T(1,128)}) custom-call(bf16[256,1024]{1,0:T(8,128)(2,1)S(1)} %get-tuple-element.438.own.final, bf16[1664,1024]{1,0:T(8,128)(2,1)} %get-tuple-element.439.tab_a, bf16[1024,1664]{1,0:T(8,128)(2,1)} %get-tuple-element.440.turn_a, bf16[1664,1024]{1,0:T(8,128)(2,1)} %get-tuple-element.441.tab_b, ...), custom_call_target="tpu_custom_call" | custom-call | tf_op jit(solution)/shard_map/cond/branch_0_fun/head/pallas_call | solution.py:817
  422.5 0.8 copy.133.mask_col
  423.3 25.5 %backward.1 = (f32[32,1024]{1,0:T(8,128)}, f32[1,128]{1,0:T(1,128)}) custom-call(bf16[1024,256]{1,0:T(8,128)(2,1)} %get-tuple-element.443.mean_rows, f32[1,256]{1,0:T(1,128)} %get-tuple-element.444.log_total, f32[1,256]{1,0:T(1,128)} %bitcast.335, f32[256,1]{1,0:T(8,128)} %copy.133.mask_col, f32[256,1024]{1,0:T(8,128)S(1)} %copy-done.19, ...), custom_call_target="tpu_custom_call" | custom-call | tf_op jit(solution)/shard_map/cond/branch_0_fun/backward/pallas_call | solution.py:1266
  448.8 0.7 pad.8.clone
  449.5 0.9 pad_maximum_fusion
  450.4 0.8 broadcast_in_dim.89.grads
  451.2 0.7 reshape.288.momenta
  451.9 22.4 %update.1 = (f32[32,256]{1,0:T(8,128)}, f32[32,256]{1,0:T(8,128)}, f32[1,128]{1,0:T(1,128)}) custom-call(f32[32,1,1152]{2,1,0:T(1,128)} %broadcast_in_dim.89.grads, f32[32,1024]{1,0:T(8,128)} %reshape.288.momenta, f32[32,1024]{1,0:T(8,128)S(1)} %get-tuple-element.449.adapters.weights), custom_call_target="tpu_custom_call" | custom-call | tf_op jit(solution)/shard_map/cond/branch_0_fun/update/pallas_call | solution.py:914
  474.3 0.8 fusion.169
  475.0 0.6 squeeze.93
  475.6 0.6 squeeze.94
  476.3 1.4 fusion.171
  477.7 0.7 copy.233
  478.4 0.7 copy.234
  488.9 0.6 convert_element_type.316
  489.5 0.6 convert_element_type.317
  (27 shorter events, 0.1 us)
Async XLA Ops:
  7.2 180.7 %copy-start.38 = (bf16[192,32]{0,1:T(8,128)(2,1)S(1)}, bf16[192,32]{0,1:T(8,128)(2,1)}, u32[]{:S(2)}) copy-start(bf16[192,32]{0,1:T(8,128)(2,1)} %param.30) | copy-start | bytes 36868
  7.2 180.7 %copy-start.67 = (bf16[288]{0:T(512)(128)(2,1)S(1)}, bf16[288]{0:T(512)(128)(2,1)}, u32[]{:S(2)}) copy-start(bf16[288]{0:T(512)(128)(2,1)} %param.37) | copy-start | bytes 1732
  7.2 180.7 %copy-start.70 = (s32[256]{0:T(256)S(1)}, s32[256]{0:T(256)}, u32[]{:S(2)}) copy-start(s32[256]{0:T(256)} %param.25) | copy-start | bytes 3076
  7.2 180.7 %copy-start.62 = (s32[256]{0:T(256)S(1)}, s32[256]{0:T(256)}, u32[]{:S(2)}) copy-start(s32[256]{0:T(256)} %param.27) | copy-start | bytes 3076
  7.2 180.7 %copy-start.23 = (f32[4,1024,4]{1,2,0:T(4,128)S(1)}, f32[4,1024,4]{1,2,0:T(4,128)}, u32[]{:S(2)}) copy-start(f32[4,1024,4]{1,2,0:T(4,128)} %param.38) | copy-start | bytes 196612
  7.2 180.7 %copy-start.20 = (f32[4,4,1024]{2,1,0:T(4,128)S(1)}, f32[4,4,1024]{2,1,0:T(4,128)}, u32[]{:S(2)}) copy-start(f32[4,4,1024]{2,1,0:T(4,128)} %refs_9_.1) | copy-start | bytes 196612
  7.2 180.7 %copy-start.26 = (f32[4,1024,4]{1,2,0:T(4,128)S(1)}, f32[4,1024,4]{1,2,0:T(4,128)}, u32[]{:S(2)}) copy-start(f32[4,1024,4]{1,2,0:T(4,128)} %param.40) | copy-start | bytes 196612
  7.3 180.7 %copy-start.29 = (f32[4,4,1024]{2,1,0:T(4,128)S(1)}, f32[4,4,1024]{2,1,0:T(4,128)}, u32[]{:S(2)}) copy-start(f32[4,4,1024]{2,1,0:T(4,128)} %param.41) | copy-start | bytes 196612
  188.0 235.3 %copy-start.19 = (f32[256,1024]{1,0:T(8,128)S(1)}, f32[256,1024]{1,0:T(8,128)}, u32[]{:S(2)}) copy-start(f32[256,1024]{1,0:T(8,128)} %get-tuple-element.446.target_rows) | copy-start | bytes 3145732
  422.5 0.8 copy-start.53
  488.9 1.2 copy-start.51
  488.9 1.2 copy-start.52
